TPU v7x, 32 devices: a whole 2x2x4 slice. The times are simulated.
32 devices in a mesh: seq: 16 (over z, y, core), ffn: 2 (over x).
Axes of the slice: x: 2, y: 2, z: 4, core: 2. Of those that a mesh axis runs over, the one named last changes fastest.
Arguments:
- tokens: bfloat16 [16384, 1024], P(('seq', 'ffn')), may hold values from -6 to 6
- spots: int32 [32, 128], P(('seq', 'ffn')), may hold values from 0 to 511, as said below
- counts: int32 [32], P(('seq', 'ffn')), may hold values from 42 to 128, as said below
- fill: bfloat16 [32, 128, 1024], P(('seq', 'ffn')), may hold values from -6 to 6
- cot: bfloat16 [32, 128, 1024], P(('seq', 'ffn')), may hold values from -6 to 6
- w_qkv: bfloat16 [1024, 3072], replicated, may hold values from -0.25 to 0.25
- b_q: bfloat16 [1024], replicated, may hold values from -3 to 3
- b_v: bfloat16 [1024], replicated, may hold values from -3 to 3
- w_out: bfloat16 [1024, 1024], replicated, may hold values from -0.375 to 0.375
- b_out: bfloat16 [1024], replicated, may hold values from -3 to 3
- gain_one: bfloat16 [1024], replicated, may hold values from 0.5 to 1.5
- shift_one: bfloat16 [1024], replicated, may hold values from -2 to 2
- w_up: bfloat16 [1024, 4096], P(None, 'ffn'), may hold values from -0.1875 to 0.1875
- b_up: bfloat16 [4096], P('ffn'), may hold values from -3 to 3
- w_down: bfloat16 [4096, 1024], P('ffn'), may hold values from -0.09375 to 0.09375
- b_down: bfloat16 [1024], replicated, may hold values from -3 to 3
- gain_two: bfloat16 [1024], replicated, may hold values from 0.5 to 1.5
- shift_two: bfloat16 [1024], replicated, may hold values from -2 to 2
Outputs:
- output: bfloat16 [16384, 1024], P(('seq', 'ffn'))
- grad_tokens: bfloat16 [16384, 1024], P(('seq', 'ffn'))
- grad_fill: bfloat16 [32, 128, 1024], P(('seq', 'ffn'))
- grad_w_qkv: float32 [1024, 3072], P('seq', 'ffn')
- grad_b_q: float32 [1024], replicated
- grad_b_v: float32 [1024], replicated
- grad_w_out: float32 [1024, 1024], P('seq', 'ffn')
- grad_b_out: float32 [1024], replicated
- grad_gain_one: float32 [1024], replicated
- grad_shift_one: float32 [1024], replicated
- grad_w_up: float32 [1024, 4096], P('seq', 'ffn')
- grad_b_up: float32 [4096], replicated
- grad_w_down: float32 [4096, 1024], P('ffn', 'seq')
- grad_b_down: float32 [1024], replicated
- grad_gain_two: float32 [1024], replicated
- grad_shift_two: float32 [1024], replicated
Inputs may be any that keep to these rules, and one draw needn't show every extreme that they name: `spots`: in row s the first counts[s] entries are distinct positions of protein s; the other entries are 0. `counts`: some protein has exactly 128 listed positions and some exactly 42.
All inputs are finite; a program needn't handle non-finite values.
Results may differ from a plain program's by a relative error of at most 0.019.
Values may be sent and summed in bfloat16 or wider, within the bound.
No kernel may reach another device: no remote copies, remote signals or barrier semaphores. Data moves between devices by JAX's collectives and lax.ppermute only.
A program may use at most 192 MiB of HBM per device.

v0:
```python
import jax
import jax.numpy as jnp
from jax import lax
from jax.sharding import PartitionSpec as P

H = 16


exact_erf_mode = lax.Precision.HIGHEST
epsilon = 1e-12


def layer_norm(value, gain, shift):
    centre = value - jnp.mean(value, axis=-1, keepdims=True)
    spread = jnp.mean(centre * centre, axis=-1, keepdims=True)
    return centre * lax.rsqrt(spread + epsilon) * gain + shift


def gelu_exact(value):
    return jax.nn.gelu(value, approximate=False)


def dot_plain(left, right):
    return jnp.dot(left, right, preferred_element_type=jnp.float32)


def dot_first(left, right):
    return lax.dot_general(
        left, right, (((0,), (0,)), ((), ())), preferred_element_type=jnp.float32
    )


def dot_second(left, right):
    return lax.dot_general(
        left, right, (((1,), (1,)), ((), ())), preferred_element_type=jnp.float32
    )


def on_device(
    tokens,
    spots,
    counts,
    fill,
    cot,
    w_qkv,
    b_q,
    b_v,
    w_out,
    b_out,
    gain_one,
    shift_one,
    w_up,
    b_up,
    w_down,
    b_down,
    gain_two,
    shift_two,
):
    local_sequences, slots = spots.shape
    sequence_length = tokens.shape[0] // local_sequences
    model_width = tokens.shape[1]
    heads = H
    head_size = model_width // heads
    scale = head_size ** (-0.5)
    positions = jnp.arange(sequence_length, dtype=jnp.int32)
    slot_ids = jnp.arange(slots, dtype=jnp.int32)
    placed_tokens = (
        (spots[:, :, None] == positions[None, None, :])
        & (slot_ids[None, :, None] < counts[:, None, None])
    ).astype(jnp.float32)
    kept = 1.0 - jnp.sum(placed_tokens, axis=1)

    def spread_rows(token_rows):
        return jnp.einsum(
            "rkx,rku->rxu", placed_tokens, token_rows, precision=exact_erf_mode
        ).reshape(-1, model_width)

    gain_a = gain_one.astype(jnp.float32)
    shift_a = shift_one.astype(jnp.float32)
    gain_b = gain_two.astype(jnp.float32)
    shift_b = shift_two.astype(jnp.float32)
    x = (
        tokens.astype(jnp.float32).reshape(local_sequences, sequence_length, model_width)
        * kept[..., None]
    ).reshape(-1, model_width) + spread_rows(fill.astype(jnp.float32))
    x_low = x.astype(jnp.bfloat16)
    bias_cat = jnp.concatenate(
        [b_q.astype(jnp.float32), jnp.zeros((model_width,), jnp.float32), b_v.astype(jnp.float32)]
    )
    qkv_low = (dot_plain(x_low, w_qkv) + bias_cat).astype(jnp.bfloat16)
    per_seq = qkv_low.reshape(local_sequences, sequence_length, 3, heads, head_size)

    def attend(block):
        query = block[:, 0]
        key_part = block[:, 1]
        value = block[:, 2]
        scores = (
            jnp.einsum("lhe,mhe->hlm", query, key_part, preferred_element_type=jnp.float32) * scale
        )
        peak = jnp.max(scores, axis=-1, keepdims=True)
        expo = jnp.exp(scores - peak)
        total = jnp.sum(expo, axis=-1, keepdims=True)
        probs = expo / total
        mixed_heads = jnp.einsum(
            "hlm,mhe->lhe", probs.astype(jnp.bfloat16), value, preferred_element_type=jnp.float32
        )
        return (
            mixed_heads.reshape(sequence_length, model_width),
            peak[..., 0] + jnp.log(total[..., 0]),
        )

    attended, log_totals = lax.map(attend, per_seq)
    att_low = attended.reshape(-1, model_width).astype(jnp.bfloat16)
    resid_one = x + dot_plain(att_low, w_out) + b_out.astype(jnp.float32)
    normed_one, pull_one = jax.vjp(layer_norm, resid_one, gain_a, shift_a)
    normed_low = normed_one.astype(jnp.bfloat16)
    up_now, down_now, bias_low = (
        lax.all_gather(w_up, "ffn", axis=1, tiled=True),
        lax.all_gather(w_down, "ffn", axis=0, tiled=True),
        lax.all_gather(b_up, "ffn", axis=0, tiled=True),
    )
    bias_now = bias_low.astype(jnp.float32)
    pre = dot_plain(normed_low, up_now) + bias_now
    hidden = gelu_exact(pre).astype(jnp.bfloat16)
    mixed = dot_plain(hidden, down_now)
    resid_two = normed_one + mixed + b_down.astype(jnp.float32)
    normed_two, pull_two = jax.vjp(layer_norm, resid_two, gain_b, shift_b)
    output = normed_two.astype(jnp.bfloat16)
    out_grad = spread_rows(cot.astype(jnp.float32))
    g_resid_two, grad_gain_two, grad_shift_two = pull_two(out_grad)
    grad_b_down = jnp.sum(g_resid_two, axis=0)
    g_down_low = g_resid_two.astype(jnp.bfloat16)
    got_rows, got_pre, got_hidden = (normed_low, pre, hidden)
    g_hidden = dot_second(g_down_low, down_now)
    gelu_out, gelu_pull = jax.vjp(gelu_exact, got_pre)
    (g_pre,) = gelu_pull(g_hidden)
    grad_b_up_part = jnp.sum(g_pre, axis=0)
    g_pre_low = g_pre.astype(jnp.bfloat16)
    grad_w_up = dot_first(got_rows, g_pre_low)
    grad_w_down = dot_first(got_hidden, g_down_low)
    g_ffn = dot_second(g_pre_low, up_now)
    g_normed = g_resid_two + g_ffn
    g_resid_one, grad_gain_one, grad_shift_one = pull_one(g_normed)
    grad_b_out = jnp.sum(g_resid_one, axis=0)
    g_attn_low = g_resid_one.astype(jnp.bfloat16)
    grad_w_out = dot_first(att_low, g_attn_low)
    g_attended = dot_second(g_attn_low, w_out).astype(jnp.bfloat16)

    def attend_back(items):
        block, g_heads, log_total = items
        query = block[:, 0]
        key_part = block[:, 1]
        value = block[:, 2]
        scores = (
            jnp.einsum("lhe,mhe->hlm", query, key_part, preferred_element_type=jnp.float32) * scale
        )
        probs = jnp.exp(scores - log_total[:, :, None])
        g_value = jnp.einsum(
            "hlm,lhe->mhe", probs.astype(jnp.bfloat16), g_heads, preferred_element_type=jnp.float32
        )
        g_probs = jnp.einsum("lhe,mhe->hlm", g_heads, value, preferred_element_type=jnp.float32)
        inner = jnp.sum(probs * g_probs, axis=-1, keepdims=True)
        g_scores = (probs * (g_probs - inner)).astype(jnp.bfloat16)
        g_query = (
            jnp.einsum("hlm,mhe->lhe", g_scores, key_part, preferred_element_type=jnp.float32)
            * scale
        )
        g_key = (
            jnp.einsum("hlm,lhe->mhe", g_scores, query, preferred_element_type=jnp.float32) * scale
        )
        return (
            jnp.stack([g_query, g_key, g_value], axis=1)
            .astype(jnp.bfloat16)
            .reshape(sequence_length, 3 * model_width)
        )

    g_qkv = lax.map(
        attend_back,
        (
            per_seq,
            g_attended.reshape(local_sequences, sequence_length, heads, head_size),
            log_totals,
        ),
    ).reshape(-1, 3 * model_width)
    grad_w_qkv = dot_first(x_low, g_qkv)
    column_sums = jnp.sum(g_qkv, axis=0, dtype=jnp.float32)
    grad_b_q = column_sums[:model_width]
    grad_b_v = column_sums[2 * model_width :]
    input_gradient = g_resid_one + dot_second(g_qkv, w_qkv)
    grad_tokens = (
        (input_gradient.reshape(local_sequences, sequence_length, model_width) * kept[..., None])
        .reshape(-1, model_width)
        .astype(jnp.bfloat16)
    )
    grad_fill = jnp.einsum(
        "fqz,fzn->fqn",
        placed_tokens,
        input_gradient.reshape(local_sequences, sequence_length, model_width),
        precision=exact_erf_mode,
    ).astype(jnp.bfloat16)
    seq_qkv, seq_out, seq_up, seq_down = (
        lax.psum_scatter(
            grad_w_qkv.astype(jnp.bfloat16), "seq", scatter_dimension=0, tiled=True
        ).astype(jnp.float32),
        lax.psum_scatter(
            grad_w_out.astype(jnp.bfloat16), "seq", scatter_dimension=0, tiled=True
        ).astype(jnp.float32),
        lax.psum_scatter(
            grad_w_up.astype(jnp.bfloat16), "seq", scatter_dimension=0, tiled=True
        ).astype(jnp.float32),
        lax.psum_scatter(
            grad_w_down.astype(jnp.bfloat16), "seq", scatter_dimension=1, tiled=True
        ).astype(jnp.float32),
    )
    final_qkv, final_out, final_up, final_down = (
        lax.psum_scatter(
            seq_qkv.astype(jnp.bfloat16), "ffn", scatter_dimension=1, tiled=True
        ).astype(jnp.float32),
        lax.psum_scatter(
            seq_out.astype(jnp.bfloat16), "ffn", scatter_dimension=1, tiled=True
        ).astype(jnp.float32),
        lax.psum_scatter(
            seq_up.astype(jnp.bfloat16), "ffn", scatter_dimension=1, tiled=True
        ).astype(jnp.float32),
        lax.psum_scatter(
            seq_down.astype(jnp.bfloat16), "ffn", scatter_dimension=0, tiled=True
        ).astype(jnp.float32),
    )
    sums = lax.psum(
        (
            grad_b_q,
            grad_b_v,
            grad_b_out,
            grad_gain_one,
            grad_shift_one,
            grad_b_up_part,
            grad_b_down,
            grad_gain_two,
            grad_shift_two,
        ),
        ("seq", "ffn"),
    )
    return (
        output,
        grad_tokens,
        grad_fill,
        final_qkv,
        sums[0],
        sums[1],
        final_out,
        sums[2],
        sums[3],
        sums[4],
        final_up,
        sums[5],
        final_down,
        sums[6],
        sums[7],
        sums[8],
    )


def solution(mesh):
    in_specs = (
        P(("seq", "ffn"), None),
        P(("seq", "ffn"), None),
        P(("seq", "ffn")),
        P(("seq", "ffn"), None, None),
        P(("seq", "ffn"), None, None),
        P(),
        P(),
        P(),
        P(),
        P(),
        P(),
        P(),
        P(None, "ffn"),
        P("ffn"),
        P("ffn", None),
        P(),
        P(),
        P(),
    )
    out_specs = (
        P(("seq", "ffn"), None),
        P(("seq", "ffn"), None),
        P(("seq", "ffn"), None, None),
        P("seq", "ffn"),
        P(),
        P(),
        P("seq", "ffn"),
        P(),
        P(),
        P(),
        P("seq", "ffn"),
        P(),
        P("ffn", "seq"),
        P(),
        P(),
        P(),
    )
    return jax.shard_map(
        on_device, mesh=mesh, in_specs=in_specs, out_specs=out_specs, check_vma=False
    )
```

profile of v0, /device:TPU:0, one launch (start us, length us, event | category | flops | bytes accessed | tf_op | source)
XLA Modules:
  0.0 705.3 jit_solution(14689181482416748100)
XLA Ops:
  12.1 7.6 %add_convert_fusion = bf16[512,3072]{1,0:T(8,128)(2,1)} fusion(bf16[1024,3072]{1,0:T(8,128)(2,1)} %param.23, f32[3072]{0:T(1024)S(1)} %pad_maximum_fusion, f32[512,1024]{1,0:T(8,128)S(1)} %multiply_add_fusion.2), kind=kOutput, calls=%fused_computation.33 | convolution fusion | flops 3224895488 | bytes 11546624 | tf_op jit(solution)/shard_map/dot_general | solution.py:24
  19.7 5.0 copy.55
  24.6 10.3 %multiply_reduce_fusion.1 = (f32[16,512]{1,0:T(8,128)S(1)}, f32[16,512,512]{1,2,0:T(8,128)}) fusion(bf16[512,3,16,64]{0,3,2,1:T(8,128)(2,1)} %bitcast.76), kind=kOutput, calls=%fused_computation.6 | convolution fusion | flops 545251328 | bytes 18907136 | tf_op jit(solution)/shard_map/while/body/eval_jaxpr/lhe,mhe->hlm/dot_general | solution.py:98
  34.9 8.6 %fusion = f32[16,512]{1,0:T(8,128)S(1)} fusion(f32[16,512,512]{1,2,0:T(8,128)} %get-tuple-element.70, f32[16,512]{1,0:T(8,128)S(1)} %get-tuple-element.69), kind=kLoop, calls=%fused_computation.5 | loop fusion | flops 12574720 | bytes 16842752 | tf_op jit(solution)/shard_map/while/body/eval_jaxpr/reduce_sum | solution.py:102
  43.6 8.1 %fusion.22 = bf16[16,64,512]{2,1,0:T(8,128)(2,1)S(1)} fusion(f32[16,512,512]{1,2,0:T(8,128)} %get-tuple-element.70, f32[16,512]{1,0:T(8,128)S(1)} %fusion, f32[16,512]{1,0:T(8,128)S(1)} %get-tuple-element.69, bf16[512,3,16,64]{0,3,2,1:T(8,128)(2,1)} %bitcast.77), kind=kOutput, calls=%fused_computation.63 | convolution fusion | flops 554172416 | bytes 18939904 | tf_op jit(solution)/shard_map/while/body/eval_jaxpr/hlm,mhe->lhe/dot_general | solution.py:104
  55.0 5.1 all_gather.10
  60.1 56.4 %all-gather.3.cloned.1.call-done = bf16[1024,4096]{1,0:T(8,128)(2,1)} async-done(((bf16[1024,2048]{1,0:T(8,128)(2,1)}), bf16[1024,4096]{1,0:T(8,128)(2,1)}) %all-gather.3.cloned.1.call-update) | async-done | bytes 8388624 | tf_op jit(solution)/shard_map/all_gather | solution.py:118
  116.5 27.9 %multiply_convert_fusion.1 = (bf16[512,4096]{1,0:T(8,128)(2,1)}, f32[512,4096]{1,0:T(8,128)}, f32[512,4096]{1,0:T(8,128)}) fusion(f32[4096]{0:T(1024)S(1)} %convert_element_type.165, bf16[1024,4096]{1,0:T(8,128)(2,1)} %all-gather.3.cloned.1.call-done, f32[512,1024]{1,0:T(8,128)} %copy-done.4, f32[1024]{0:T(1024)S(1)} %convert_element_type.163, ...), kind=kOutput, calls=%fused_computation.13 | convolution fusion | flops 4436000768 | bytes 31485952 | tf_op jit(solution)/shard_map/dot_general | solution.py:24
  144.3 77.7 %all-gather.5.cloned.1.call-done = bf16[4096,1024]{1,0:T(8,128)(2,1)} async-done(((bf16[2048,1024]{1,0:T(8,128)(2,1)}), bf16[4096,1024]{1,0:T(8,128)(2,1)}) %all-gather.5.cloned.1.call-update) | async-done | bytes 8388624 | tf_op jit(solution)/shard_map/all_gather | solution.py:119
  222.0 9.9 %fusion.57 = (f32[512]{0:T(512)S(1)}, f32[512,1024]{1,0:T(8,128)S(1)}) fusion(f32[1024]{0:T(1024)S(1)} %convert_element_type.167, bf16[512,4096]{1,0:T(8,128)(2,1)} %get-tuple-element.64, bf16[4096,1024]{1,0:T(8,128)(2,1)} %all-gather.5.cloned.1.call-done, f32[1024]{0:T(1024)S(1)} %convert_element_type.163, f32[1024]{0:T(1024)S(1)} %convert_element_type.162, ...), kind=kOutput, calls=%fused_computation.113 | convolution fusion | flops 4298636800 | bytes 16795648 | tf_op jit(solution)/shard_map/dot_general | solution.py:24
  233.4 1.8 fusion.53
  235.2 15.9 %fusion.58 = (f32[4096]{0:T(1024)S(1)}, bf16[512,4096]{1,0:T(8,128)(2,1)}) fusion(f32[512,4096]{1,0:T(8,128)} %get-tuple-element.65, bf16[4096,1024]{1,0:T(8,128)(2,1)} %all-gather.5.cloned.1.call-done, f32[512,1024]{1,0:T(8,128)S(1)} %get-tuple-element.63, f32[512]{0:T(512)S(1)} %negate_multiply_fusion.2, f32[512,4096]{1,0:T(8,128)} %get-tuple-element.73, ...), kind=kOutput, calls=%fused_computation.114 | convolution fusion | flops 4329566208 | bytes 31492096 | tf_op jit(solution)/shard_map/dot_general | solution.py:34
  251.1 9.0 %multiply_reduce_fusion.3 = (f32[1024]{0:T(1024)S(1)}, f32[512]{0:T(512)S(1)}, f32[1024]{0:T(1024)S(1)}, f32[512,1024]{1,0:T(8,128)S(1)}) fusion(f32[512,1024]{1,0:T(8,128)S(1)} %copy-done.5, f32[512]{0:T(512)S(1)} %fusion.44, f32[512]{0:T(512)S(1)} %broadcast_multiply_fusion.1, f32[1024]{0:T(1024)S(1)} %convert_element_type.162, ...), kind=kOutput, calls=%fused_computation.38 | convolution fusion | flops 4300207616 | bytes 18894848 | tf_op jit(solution)/shard_map/dot_general | solution.py:34
  262.2 2.7 convolution_convert_fusion.3
  264.9 3.9 convolution_convert_fusion.4
  268.8 1.9 copy.57
  270.7 11.9 %multiply_reduce_fusion = (f32[16,512]{1,0:T(8,128)S(1)}, f32[16,512,512]{1,2,0:T(8,128)}) fusion(f32[16,512,512]{1,2,0:T(8,128)} %get-tuple-element.70, f32[16,512]{1,0:T(8,128)S(1)} %log_add_fusion, bf16[512,16,64]{0,2,1:T(8,128)(2,1)S(1)} %bitcast.81, bf16[512,3,16,64]{0,3,2,1:T(8,128)(2,1)} %bitcast.78), kind=kOutput, calls=%fused_computation.1 | convolution fusion | flops 553639936 | bytes 35717120 | tf_op jit(solution)/shard_map/while/body/eval_jaxpr/lhe,mhe->hlm/dot_general | solution.py:161
  282.6 12.4 %multiply_convert_fusion = bf16[16,512,512]{1,2,0:T(8,128)(2,1)S(1)} fusion(f32[16,512,512]{1,2,0:T(8,128)} %get-tuple-element.79, f32[16,512,512]{1,2,0:T(8,128)} %get-tuple-element.70, f32[16,512]{1,0:T(8,128)S(1)} %get-tuple-element.78, f32[16,512]{1,0:T(8,128)S(1)} %log_add_fusion), kind=kLoop, calls=%fused_computation | loop fusion | flops 20971520 | bytes 42008576 | tf_op jit(solution)/shard_map/while/body/eval_jaxpr/convert_element_type | solution.py:163
  295.0 2.6 multiply_bitcast_fusion
  299.1 7.5 %fusion.17 = bf16[512,1,16,64]{0,3,2,1:T(8,128)(2,1)S(1)} fusion(bf16[512,16,64]{0,2,1:T(8,128)(2,1)S(1)} %bitcast.82, f32[16,512,512]{1,2,0:T(8,128)} %get-tuple-element.70, f32[16,512]{1,0:T(8,128)S(1)} %log_add_fusion), kind=kOutput, calls=%fused_computation.62 | convolution fusion | flops 549453824 | bytes 18907136 | tf_op jit(solution)/shard_map/while/body/eval_jaxpr/hlm,lhe->mhe/dot_general | solution.py:158
  309.0 5.5 convolution_convert_fusion.2
  314.7 10.8 %convolution_convert_fusion.1 = bf16[1024,4096]{1,0:T(8,128)(2,1)} fusion(bf16[512,4096]{1,0:T(8,128)(2,1)} %get-tuple-element.83, f32[512,1024]{1,0:T(8,128)} %copy-done.4, f32[1024]{0:T(1024)S(1)} %convert_element_type.163, f32[1024]{0:T(1024)S(1)} %convert_element_type.162, f32[512]{0:T(512)S(1)} %fusion.44, f32[512]{0:T(512)S(1)} %broadcast_multiply_fusion.1), kind=kOutput, calls=%fused_computation.30 | convolution fusion | flops 4301783040 | bytes 14692352 | tf_op jit(solution)/shard_map/dot_general | solution.py:28
  325.6 10.7 %convolution_convert_fusion = bf16[4096,1024]{0,1:T(8,128)(2,1)} fusion(bf16[512,4096]{1,0:T(8,128)(2,1)} %get-tuple-element.64, f32[512,1024]{1,0:T(8,128)} %copy-done.2, f32[512]{0:T(512)S(1)} %negate_multiply_fusion.2), kind=kOutput, calls=%fused_computation.29 | convolution fusion | flops 4300210176 | bytes 14682112 | tf_op jit(solution)/shard_map/dot_general | solution.py:28
  337.2 81.9 %reduce-scatter.9.cloned.1.call-done = bf16[64,3072]{1,0:T(8,128)(2,1)} async-done(((bf16[1024,3072]{1,0:T(8,128)(2,1)}), bf16[64,3072]{1,0:T(8,128)(2,1)}) %reduce-scatter.9.cloned.1.call-update) | async-done | bytes 393232 | tf_op jit(solution)/shard_map/reduce_scatter | solution.py:202
  419.1 107.8 %reduce-scatter.17.cloned.1.call-done = bf16[64,4096]{1,0:T(8,128)(2,1)} async-done(((bf16[1024,4096]{1,0:T(8,128)(2,1)}), bf16[64,4096]{1,0:T(8,128)(2,1)}) %reduce-scatter.17.cloned.1.call-update) | async-done | bytes 524304 | tf_op jit(solution)/shard_map/reduce_scatter | solution.py:208
  528.9 1.8 add_reduce_fusion.1
  530.7 42.2 %all-reduce = (f32[1024]{0:T(1024)}, f32[1024]{0:T(1024)}, f32[1024]{0:T(1024)}, f32[1024]{0:T(1024)}, f32[1024]{0:T(1024)}, /*index=5*/f32[4096]{0:T(1024)}, f32[1024]{0:T(1024)}, f32[1024]{0:T(1024)}, f32[1024]{0:T(1024)}) all-reduce(f32[1024]{0:T(1024)S(1)} %slice.34, ...), channel_id=1, replica_groups=mesh['seq'=16,'ffn'=2] {'seq','ffn'}, use_global_device_ids=true, to_apply=%region_15.16 | all-reduce | flops 12288 | bytes 98304 | tf_op jit(solution)/shard_map/psum | solution.py:229
  572.9 62.3 %reduce-scatter.21.cloned.1.call-done = bf16[4096,64]{0,1:T(8,128)(2,1)} async-done(((bf16[4096,1024]{0,1:T(8,128)(2,1)}), bf16[4096,64]{0,1:T(8,128)(2,1)}) %reduce-scatter.21.cloned.1.call-update) | async-done | bytes 524304 | tf_op jit(solution)/shard_map/reduce_scatter | solution.py:211
  635.3 8.9 %multiply_convert_fusion.2 = (bf16[512,1024]{1,0:T(8,128)(2,1)}, f32[512,1024]{1,0:T(8,128)S(1)}) fusion(f32[512]{0:T(512)S(1)} %copy-done.14, bf16[512,3072]{0,1:T(8,128)(2,1)} %bitcast.84, bf16[1024,3072]{1,0:T(8,128)(2,1)} %param.23, f32[512,1024]{1,0:T(8,128)} %copy-done.3, f32[512]{0:T(512)S(1)} %negate_multiply_fusion.1), kind=kOutput, calls=%fused_computation.39 | convolution fusion | flops 3223322624 | bytes 14684160 | tf_op jit(solution)/shard_map/dot_general | solution.py:34
  649.0 13.9 %reduce-scatter.11.cloned.1.call-done = bf16[64,1536]{1,0:T(8,128)(2,1)} async-done(((bf16[64,3072]{1,0:T(8,128)(2,1)}), bf16[64,1536]{1,0:T(8,128)(2,1)}) %reduce-scatter.11.cloned.1.call-update) | async-done | bytes 196624 | tf_op jit(solution)/shard_map/reduce_scatter | solution.py:216
  664.6 15.2 %reduce-scatter.19.cloned.1.call-done = bf16[64,2048]{1,0:T(8,128)(2,1)} async-done(((bf16[64,4096]{1,0:T(8,128)(2,1)}), bf16[64,2048]{1,0:T(8,128)(2,1)}) %reduce-scatter.19.cloned.1.call-update) | async-done | bytes 262160 | tf_op jit(solution)/shard_map/reduce_scatter | solution.py:222
  681.6 14.9 %reduce-scatter.23.cloned.1.call-done = bf16[2048,64]{0,1:T(8,128)(2,1)} async-done(((bf16[4096,64]{0,1:T(8,128)(2,1)}), bf16[2048,64]{0,1:T(8,128)(2,1)}) %reduce-scatter.23.cloned.1.call-update) | async-done | bytes 262160 | tf_op jit(solution)/shard_map/reduce_scatter | solution.py:225
  (116 shorter events, 27.7 us)
Async XLA Ops:
  7.2 44.5 %copy-start = (bf16[1024,1024]{1,0:T(8,128)(2,1)S(1)}, bf16[1024,1024]{1,0:T(8,128)(2,1)}, u32[]{:S(2)}) copy-start(bf16[1024,1024]{1,0:T(8,128)(2,1)} %param.26) | copy-start | bytes 6291460
  7.2 2.2 copy-start.15
  7.2 2.4 copy-start.17
  7.2 2.4 copy-start.18
  7.2 2.9 copy-start.12
  7.2 2.9 copy-start.10
  7.2 109.2 %all-gather.3.cloned.1.call-start = ((), (), s32[]{:S(2)}) async-start(), calls=%async_computation.8 | async-start | bytes 12582912 | tf_op jit(solution)/shard_map/all_gather | solution.py:118
  8.0 214.1 %all-gather.5.cloned.1.call-start = ((), (), s32[]{:S(2)}) async-start(), calls=%async_computation.9 | async-start | bytes 12582912 | tf_op jit(solution)/shard_map/all_gather | solution.py:119
  8.7 327.7 %reduce-scatter.13.cloned.1.call-start = ((), (), s32[]{:S(2)}) async-start(), calls=%async_computation.12 | async-start | bytes 2228224 | tf_op jit(solution)/shard_map/reduce_scatter | solution.py:205
  43.5 8.1 %copy-start.19 = (bf16[1024]{0:T(1024)(128)(2,1)S(1)}, bf16[1024]{0:T(1024)(128)(2,1)}, u32[]{:S(2)}) copy-start(bf16[1024]{0:T(1024)(128)(2,1)} %param.27) | copy-start | bytes 6148
  43.6 8.2 %copy-start.8 = (f32[512,1024]{1,0:T(8,128)S(1)}, f32[512,1024]{1,0:T(8,128)}, u32[]{:S(2)}) copy-start(f32[512,1024]{1,0:T(8,128)} %copy-done.7) | copy-start | bytes 6291460
  51.7 3.2 copy-start.20
  51.7 3.2 copy-start.21
  51.7 3.2 copy-start.22
  51.8 3.2 copy-start.23
  51.8 3.2 copy-start.24
  51.8 3.2 copy-start.16
  222.0 10.3 %copy-start.11 = (bf16[1,128,1024]{2,1,0:T(8,128)(2,1)S(1)}, bf16[1,128,1024]{2,1,0:T(8,128)(2,1)}, u32[]{:S(2)}) copy-start(bf16[1,128,1024]{2,1,0:T(8,128)(2,1)} %param.22) | copy-start | bytes 786436
  235.2 15.9 %copy-start.2 = (f32[512,1024]{1,0:T(8,128)}, f32[512,1024]{1,0:T(8,128)S(1)}, u32[]{:S(2)}) copy-start(f32[512,1024]{1,0:T(8,128)S(1)} %get-tuple-element.63) | copy-start | bytes 6291460
  235.2 15.9 %copy-start.5 = (f32[512,1024]{1,0:T(8,128)S(1)}, f32[512,1024]{1,0:T(8,128)}, u32[]{:S(2)}) copy-start(f32[512,1024]{1,0:T(8,128)} %copy-done.4) | copy-start | bytes 6291460
  260.1 2.1 copy-start.26
  268.7 150.3 %reduce-scatter.9.cloned.1.call-start = ((), (), s32[]{:S(2)}) async-start(), calls=%async_computation.10 | async-start | bytes 6684672 | tf_op jit(solution)/shard_map/reduce_scatter | solution.py:202
  282.6 12.4 %copy-start.1 = (bf16[512,3072]{0,1:T(8,128)(2,1)S(1)}, bf16[512,3072]{0,1:T(8,128)(2,1)}, u32[]{:S(2)}) copy-start(bf16[512,3072]{0,1:T(8,128)(2,1)} %copy.55) | copy-start | bytes 9437188
  306.7 2.3 copy-start.9
  307.3 1.7 copy-start.6
  314.5 212.4 %reduce-scatter.17.cloned.1.call-start = ((), (), s32[]{:S(2)}) async-start(), calls=%async_computation.14 | async-start | bytes 8912896 | tf_op jit(solution)/shard_map/reduce_scatter | solution.py:208
  325.6 309.7 %reduce-scatter.21.cloned.1.call-start = ((), (), s32[]{:S(2)}) async-start(), calls=%async_computation.16 | async-start | bytes 8912896 | tf_op jit(solution)/shard_map/reduce_scatter | solution.py:211
  336.4 298.9 %copy-start.14 = (f32[512]{0:T(512)S(1)}, f32[512]{0:T(512)}, u32[]{:S(2)}) copy-start(f32[512]{0:T(512)} %copy-done.13) | copy-start | bytes 6148
  336.4 311.1 %reduce-scatter.15.cloned.1.call-start = ((), (), s32[]{:S(2)}) async-start(), calls=%async_computation.13 | async-start | bytes 196608 | tf_op jit(solution)/shard_map/reduce_scatter | solution.py:219
  337.1 325.7 %reduce-scatter.11.cloned.1.call-start = ((), (), s32[]{:S(2)}) async-start(), calls=%async_computation.11 | async-start | bytes 589824 | tf_op jit(solution)/shard_map/reduce_scatter | solution.py:216
  419.1 260.7 %reduce-scatter.19.cloned.1.call-start = ((), (), s32[]{:S(2)}) async-start(), calls=%async_computation.15 | async-start | bytes 786432 | tf_op jit(solution)/shard_map/reduce_scatter | solution.py:222
  526.9 169.5 %reduce-scatter.23.cloned.1.call-start = ((), (), s32[]{:S(2)}) async-start(), calls=%async_computation.17 | async-start | bytes 786432 | tf_op jit(solution)/shard_map/reduce_scatter | solution.py:225
  (5 other events, 6.1 us)
Sparse Core Ops, SparseCore 0:
  9.6 106.7 all-gather.2
  118.0 103.9 all-gather.4
  268.9 61.5 reduce-scatter.12
  334.8 84.2 reduce-scatter.8
  423.0 103.8 reduce-scatter.16
  530.8 104.3 reduce-scatter.20
  637.4 9.9 reduce-scatter.14
  649.7 13.1 reduce-scatter.10
  665.2 14.5 reduce-scatter.18
  681.9 14.5 reduce-scatter.22
where the time goes:
time: 714 us; the launch traced here: 705 us
  waiting for transfers between devices  434 us (61%)
  matrix products  159 us (22%)
  blocking collectives  47.2 us (7%)
  other arithmetic  35.4 us (5%)
  between operations  15.6 us (2%)
  local copies, waits for them, and re-layouts  13.3 us (2%)
    reduce_scatter x1, waiting for transfers between devices, on_device(): lax.psum_scatter(grad_w_up.astype(jnp.bfloat16), 'seq', scatter_dimension...  108 us
    reduce_scatter x1, waiting for transfers between devices, on_device(): lax.psum_scatter(grad_w_qkv.astype(jnp.bfloat16), 'seq', scatter_dimensio...  81.9 us
    all_gather x1, waiting for transfers between devices, on_device(): lax.all_gather(w_down, 'ffn', axis=0, tiled=True)  77.7 us
    reduce_scatter x1, waiting for transfers between devices, on_device(): lax.psum_scatter(grad_w_down.astype(jnp.bfloat16), 'seq', scatter_dimensi...  62.3 us
    all_gather x1, waiting for transfers between devices, on_device(): lax.all_gather(w_up, 'ffn', axis=1, tiled=True)  56.4 us
    dot_general x4, matrix products, dot_plain(): return jnp.dot(left, right, preferred_element_type=jnp.float32)  46.8 us
    psum x1, blocking collectives, on_device(): lax.psum((grad_b_q, grad_b_v, grad_b_out, grad_gain_one, grad_shift_one,...  42.2 us
    dot_general x4, matrix products, dot_second(): lax.dot_general(left, right, (((1,), (1,)), ((), ())), preferred_element_...  37.6 us
  transfers between devices with their start and end apart: 10, of which 9 were waited for; matrix products, arithmetic and copies ran while one was open for 22% of the time, Pallas kernels for 0%

commit v1 on v0

v1 whole, which is shorter than its diff:
```python
import functools

import jax
import jax.numpy as jnp
from jax import lax
from jax.experimental import pallas as pl
from jax.experimental.pallas import tpu as pltpu
from jax.sharding import PartitionSpec as P

H = 16
F32 = jnp.float32
LOW = jnp.bfloat16
epsilon = 1e-12
LOG2E = 1.4426950408889634
NT = (((1,), (1,)), ((), ()))
WIDE = 512
STEP = 10**11


def mm(left, right):
    return jnp.dot(left, right, preferred_element_type=F32)


def mm_nt(left, right):
    return lax.dot_general(left, right, NT, preferred_element_type=F32)


def call(body, grid, in_specs, out_specs, out_shape, scratch=(), prefetch=1, mib=48, weight=0):
    return pl.pallas_call(
        body,
        grid_spec=pltpu.PrefetchScalarGridSpec(
            num_scalar_prefetch=prefetch,
            grid=grid,
            in_specs=in_specs,
            out_specs=out_specs,
            scratch_shapes=list(scratch),
        ),
        out_shape=out_shape,
        compiler_params=pltpu.CompilerParams(
            dimension_semantics=("arbitrary",) * len(grid), vmem_limit_bytes=mib << 20
        ),
        cost_estimate=pl.CostEstimate(flops=1 + weight * STEP, bytes_accessed=1, transcendentals=0),
    )


def spec(shape, index):
    return pl.BlockSpec(shape, index)


def shape(dims, dtype):
    return jax.ShapeDtypeStruct(dims, dtype)


def one_hot_rows(sc, spots, first, rows):
    slots = spots.shape[1]
    place = lax.broadcasted_iota(jnp.int32, (rows, slots), 0) + first
    slot = lax.broadcasted_iota(jnp.int32, (rows, slots), 1)
    hit = (place == spots) & (slot < sc[2])
    return jnp.where(hit, 1.0, 0.0)


def store_turned(sc, value, keep_ref, send_ref, first_column, chunk):
    columns = value.shape[1]
    for block in range(0, columns, 128):
        turned = jnp.transpose(value[:, block : block + 128]).astype(LOW)
        for part in range(0, 128, chunk):
            place = ((first_column + block + part) // chunk) ^ sc[0]
            piece = turned[part : part + chunk]
            at = ((place // 2) % 2) * (keep_ref.shape[0] // 2) + place // 4

            @pl.when(place % 2 == 0)
            def _():
                keep_ref[at] = piece

            @pl.when(place % 2 == 1)
            def _():
                send_ref[at] = piece


def qkv_body(chunk, sc, tokens, spots, fill, w, bias, x_out, keep, send, qkv):
    @pl.when(pl.program_id(0) == 0)
    def _():
        placed = one_hot_rows(sc, spots[...], 0, tokens.shape[0])
        kept = 1.0 - jnp.sum(placed, axis=1, keepdims=True)
        x = tokens[...].astype(F32) * kept + mm(placed.astype(LOW), fill[...])
        x_out[...] = x.astype(LOW)
        store_turned(sc, x, keep, send, 0, chunk)

    qkv[...] = (mm(x_out[...], w[...]) + bias[...]).astype(LOW)


def embed_qkv(sc, tokens, spots, fill, w_qkv, bias, n_seq):
    rows, width = tokens.shape
    out = w_qkv.shape[1]
    block = 512
    chunk = width // n_seq
    turned = (n_seq // 2, chunk, rows)
    whole = lambda j, sc: (0, 0)
    return call(
        functools.partial(qkv_body, chunk),
        (out // block,),
        [
            spec((rows, width), whole),
            spec(spots.shape, whole),
            spec(fill.shape, whole),
            spec((width, block), lambda j, sc: (0, j)),
            spec((1, block), lambda j, sc: (0, j)),
        ],
        [
            spec((rows, width), whole),
            spec(turned, lambda j, sc: (0, 0, 0)),
            spec(turned, lambda j, sc: (0, 0, 0)),
            spec((rows, block), lambda j, sc: (0, j)),
        ],
        [shape((rows, width), LOW), shape(turned, LOW), shape(turned, LOW), shape((rows, out), LOW)],
    )(sc, tokens, spots, fill, w_qkv, bias)


def head_masks(width, size, factor):
    lane = lax.broadcasted_iota(jnp.int32, (1, width), 1)
    return [
        jnp.where(lane // size == n, factor, 0.0).astype(LOW) for n in range(width // size)
    ]


def attend_body(chunk, scale, sc, q, k, v, att, keep, send, logs):
    rows, width = q.shape
    size = width // 2
    masks = head_masks(width, size, scale)
    lane = lax.broadcasted_iota(jnp.int32, (1, width), 1)
    mixed, stats = [], []
    for mask in masks:
        scores = mm_nt(q[...] * mask, k[...])
        peak = jnp.max(scores, axis=1, keepdims=True) * LOG2E
        expo = jnp.exp2(scores * LOG2E - peak)
        total = jnp.sum(expo, axis=1, keepdims=True)
        mixed.append(mm(expo.astype(LOW), v[...]) / total)
        stats.append(peak + jnp.log2(total))
    both = jnp.where(lane < size, mixed[0], mixed[1])
    att[...] = both.astype(LOW)
    table = jnp.where(lane == 0, stats[0], stats[1])
    logs[0] = jnp.transpose(table)[0:2]
    place_first = pl.program_id(0) * width
    store_turned(sc, both, keep, send, place_first, chunk)


def attend(sc, qkv, n_seq):
    rows = qkv.shape[0]
    width = qkv.shape[1] // 3
    size = width // H
    pair = 2 * size
    pairs = width // pair
    chunk = width // n_seq
    turned = (n_seq // 2, chunk, rows)
    whole = lambda j, sc: (0, 0, 0)
    return call(
        functools.partial(attend_body, chunk, size ** (-0.5)),
        (pairs,),
        [
            spec((rows, pair), lambda j, sc: (0, j)),
            spec((rows, pair), lambda j, sc: (0, pairs + j)),
            spec((rows, pair), lambda j, sc: (0, 2 * pairs + j)),
        ],
        [
            spec((rows, pair), lambda j, sc: (0, j)),
            spec(turned, whole),
            spec(turned, whole),
            spec((1, 2, rows), lambda j, sc: (j, 0, 0)),
        ],
        [
            shape((rows, width), LOW),
            shape(turned, LOW),
            shape(turned, LOW),
            shape((pairs, 2, rows), F32),
        ],
    )(sc, qkv, qkv, qkv)


def norm_one_body(chunk, sc, att, w, x, b, gain, shift, hat, inv, low, keep, send):
    value = x[...].astype(F32) + mm(att[...], w[...]) + b[...]
    centre = value - jnp.mean(value, axis=-1, keepdims=True)
    spread = jnp.mean(centre * centre, axis=-1, keepdims=True)
    inverse = lax.rsqrt(spread + epsilon)
    scaled = centre * inverse
    hat[...] = scaled
    inv[...] = inverse
    normed = scaled * gain[...] + shift[...]
    low[...] = normed.astype(LOW)
    store_turned(sc, normed, keep, send, 0, chunk)


def norm_one(sc, att, w_out, x, b_out, gain, shift, n_seq):
    rows, width = x.shape
    block = 128
    chunk = width // n_seq
    turned = (n_seq // 2, chunk, rows)
    row = lambda i, sc: (i, 0)
    whole = lambda i, sc: (0, 0)
    vector = spec((1, width), whole)
    return call(
        functools.partial(norm_one_body, chunk),
        (rows // block,),
        [spec((block, width), row), spec((width, width), whole), spec((block, width), row), vector, vector, vector],
        [
            spec((block, width), row),
            spec((block, 1), row),
            spec((block, width), row),
            spec((n_seq // 2, chunk, block), lambda i, sc: (0, 0, i)),
            spec((n_seq // 2, chunk, block), lambda i, sc: (0, 0, i)),
        ],
        [
            shape((rows, width), F32),
            shape((rows, 1), F32),
            shape((rows, width), LOW),
            shape(turned, LOW),
            shape(turned, LOW),
        ],
    )(sc, att, w_out, x, b_out, gain, shift)


TAIL = tuple(0.5 * c for c in (0.254829592, -0.284496736, 1.421413741, -1.453152027, 1.061405429))
TAIL_P = 0.3275911 * 0.7071067811865476


def gelu_both(x):
    t = 1.0 / (1.0 + TAIL_P * jnp.abs(x))
    bell = jnp.exp2(x * x * (-0.5 * LOG2E))
    poly = TAIL[4]
    for c in TAIL[3::-1]:
        poly = poly * t + c
    tail = poly * t * bell
    mass = jnp.where(x < 0.0, tail, 1.0 - tail)
    return x * mass, mass + x * bell * 0.3989422804014327


def ffn_specs(split, width, part):
    if split == "own":
        ups = [spec((width, WIDE), lambda j, sc: (0, j))]
        downs = [spec((WIDE, width), lambda j, sc: (j, 0))]
        return ups, downs, WIDE
    if split == "stack":
        ups = [spec((None, width, part), lambda j, sc: (j, 0, 0))]
        downs = [spec((None, part, width), lambda j, sc: (j, 0, 0))]
        return ups, downs, part
    near = lambda j, sc: (jnp.minimum(j, 2), 0, 0)
    far = lambda j, sc: (0, 0, 0)
    ups = [spec((None, width, part), at) for at in (near, near, far, far)]
    downs = [spec((None, part, width), at) for at in (near, near, far, far)]
    return ups, downs, part


def column_block(split):
    if split == "pairs":
        return lambda j, sc: (0, j ^ ((sc[0] // 2) % 4))
    return lambda j, sc: (0, j)


def for_pieces(split, size, sc, ups, downs, work):
    if split != "pairs":
        work([(ups[0], downs[0], 0)])
        return
    core = sc[0] % 2
    places = [pl.multiple_of(core * size, size), pl.multiple_of((1 - core) * size, size)]
    step = pl.program_id(0)
    pl.when(step < 3)(lambda: work(list(zip(ups[:2], downs[:2], places))))
    pl.when(step == 3)(lambda: work(list(zip(ups[2:], downs[2:], places))))


def ffn_fwd_body(split, size, n, first, sc, *refs):
    low, bias = refs[:2]
    ups, downs = refs[2 : 2 + n], refs[2 + n : 2 + 2 * n]
    rest = refs[2 + 2 * n :]
    start = None
    if not first:
        start, rest = rest[0], rest[1:]
    hidden, slope, total = rest
    @pl.when(pl.program_id(0) == 0)
    def _():
        total[...] = jnp.zeros_like(total) if first else start[...]

    def work(pieces):
        mixed = None
        for up, down, offset in pieces:
            columns = pl.ds(offset, size)
            pre = mm(low[...], up[...]) + bias[:, columns]
            act, grad = gelu_both(pre)
            act = act.astype(LOW)
            hidden[:, columns] = act
            slope[:, columns] = grad.astype(LOW)
            product = mm(act, down[...])
            mixed = product if mixed is None else mixed + product
        total[...] += mixed

    for_pieces(split, size, sc, ups, downs, work)


def ffn_fwd(sc, low, bias, ups, downs, split, start=None):
    rows, width = low.shape
    units = bias.shape[1]
    part = ups[0].shape[-1]
    up_specs, down_specs, size = ffn_specs(split, width, part)
    step = WIDE if split != "stack" else part
    whole = lambda j, sc: (0, 0)
    column = column_block(split)
    total = spec((rows, width), whole)
    first = start is None
    return call(
        functools.partial(ffn_fwd_body, split, size, len(ups), first),
        (units // step,),
        [total, spec((1, step), column)] + up_specs + down_specs + ([] if first else [total]),
        [spec((rows, step), column), spec((rows, step), column), total],
        [shape((rows, units), LOW), shape((rows, units), LOW), shape((rows, width), F32)],
    )(sc, low, bias, *ups, *downs, *([] if first else [start]))


def ffn_bwd_body(split, size, n, first, sc, *refs):
    low, slope = refs[:2]
    ups, downs = refs[2 : 2 + n], refs[2 + n : 2 + 2 * n]
    rest = refs[2 + 2 * n :]
    start = None
    if not first:
        start, rest = rest[0], rest[1:]
    g_low, sums, total = rest
    @pl.when(pl.program_id(0) == 0)
    def _():
        total[...] = jnp.zeros_like(total) if first else start[...]

    def work(pieces):
        mixed = None
        for up, down, offset in pieces:
            columns = pl.ds(offset, size)
            g_pre = mm_nt(low[...], down[...]) * slope[:, columns].astype(F32)
            sums[:, columns] = jnp.sum(g_pre, axis=0, keepdims=True)
            rounded = g_pre.astype(LOW)
            g_low[:, columns] = rounded
            product = mm_nt(rounded, up[...])
            mixed = product if mixed is None else mixed + product
        total[...] += mixed

    for_pieces(split, size, sc, ups, downs, work)


def ffn_bwd(sc, low, slope, ups, downs, split, start=None):
    rows, width = low.shape
    units = slope.shape[1]
    part = ups[0].shape[-1]
    up_specs, down_specs, size = ffn_specs(split, width, part)
    step = WIDE if split != "stack" else part
    whole = lambda j, sc: (0, 0)
    column = column_block(split)
    total = spec((rows, width), whole)
    first = start is None
    return call(
        functools.partial(ffn_bwd_body, split, size, len(ups), first),
        (units // step,),
        [total, spec((rows, step), column)] + up_specs + down_specs + ([] if first else [total]),
        [spec((rows, step), column), spec((1, step), column), total],
        [shape((rows, units), LOW), shape((1, units), F32), shape((rows, width), F32)],
    )(sc, low, slope, *ups, *downs, *([] if first else [start]))


def norm_back(hat, inverse, gain, grad):
    inner = grad * gain
    mean = jnp.mean(inner, axis=-1, keepdims=True)
    along = jnp.mean(inner * hat, axis=-1, keepdims=True)
    return inverse * (inner - mean - hat * along)


def add_sums(sums, rows):
    @pl.when(pl.program_id(0) == 0)
    def _():
        sums[...] = jnp.zeros_like(sums)

    for n, value in enumerate(rows):
        sums[n : n + 1, :] += jnp.sum(value, axis=0, keepdims=True)


def norm_two_body(chunk, sc, mixed, hat_one, gain_one, shift_one, b_down, gain, shift, spots, cot, out, grad, low, keep, send, sums):
    rows = mixed.shape[0]
    value = hat_one[...] * gain_one[...] + shift_one[...] + mixed[...] + b_down[...]
    centre = value - jnp.mean(value, axis=-1, keepdims=True)
    spread = jnp.mean(centre * centre, axis=-1, keepdims=True)
    inverse = lax.rsqrt(spread + epsilon)
    hat = centre * inverse
    out[...] = (hat * gain[...] + shift[...]).astype(LOW)
    placed = one_hot_rows(sc, spots[...], pl.program_id(0) * rows, rows)
    out_grad = mm(placed.astype(LOW), cot[...])
    result = norm_back(hat, inverse, gain[...], out_grad)
    grad[...] = result
    low[...] = result.astype(LOW)
    store_turned(sc, result, keep, send, 0, chunk)
    add_sums(sums, (out_grad * hat, out_grad, result))


def norm_two(sc, mixed, hat_one, gain_one, shift_one, b_down, gain, shift, spots, cot, n_seq):
    rows, width = mixed.shape
    block = 128
    chunk = width // n_seq
    turned = (n_seq // 2, chunk, rows)
    row = lambda i, sc: (i, 0)
    whole = lambda i, sc: (0, 0)
    vector = spec((1, width), whole)
    tile = spec((block, width), row)
    return call(
        functools.partial(norm_two_body, chunk),
        (rows // block,),
        [tile, tile, vector, vector, vector, vector, vector, spec(spots.shape, whole), spec(cot.shape, whole)],
        [
            tile,
            tile,
            tile,
            spec((n_seq // 2, chunk, block), lambda i, sc: (0, 0, i)),
            spec((n_seq // 2, chunk, block), lambda i, sc: (0, 0, i)),
            spec((8, width), whole),
        ],
        [
            shape((rows, width), LOW),
            shape((rows, width), F32),
            shape((rows, width), LOW),
            shape(turned, LOW),
            shape(turned, LOW),
            shape((8, width), F32),
        ],
        weight=1,
    )(sc, mixed, hat_one, gain_one, shift_one, b_down, gain, shift, spots, cot)


def norm_one_back_body(sc, grad_two, ffn, hat, inv, gain, w, grad, low, g_att, sums):
    g_normed = grad_two[...] + ffn[...]
    result = norm_back(hat[...], inv[...], gain[...], g_normed)
    grad[...] = result
    rounded = result.astype(LOW)
    low[...] = rounded
    g_att[...] = mm_nt(rounded, w[...]).astype(LOW)
    add_sums(sums, (g_normed * hat[...], g_normed, result))


def norm_one_back(sc, grad_two, ffn, hat, inv, gain, w_out):
    rows, width = hat.shape
    block = 128
    row = lambda i, sc: (i, 0)
    whole = lambda i, sc: (0, 0)
    tile = spec((block, width), row)
    return call(
        norm_one_back_body,
        (rows // block,),
        [tile, tile, tile, spec((block, 1), row), spec((1, width), whole), spec((width, width), whole)],
        [tile, tile, tile, spec((8, width), whole)],
        [shape((rows, width), F32), shape((rows, width), LOW), shape((rows, width), LOW), shape((8, width), F32)],
    )(sc, grad_two, ffn, hat, inv, gain, w_out)


def attend_back_body(scale, sc, q, k, v, att, g_att, logs, g_qkv, sums):
    rows, width = q.shape
    size = width // 2
    k_all, v_all = k[...], v[...]
    ones = head_masks(width, size, 1.0)
    halves = head_masks(width, size, scale)
    inner = jnp.transpose(att[...].astype(F32) * g_att[...].astype(F32))
    k_turned = jnp.transpose(k_all.astype(F32) * scale).astype(LOW)
    g_v = g_k = None
    g_q = []
    for n in range(2):
        q_one = q[...] * halves[n]
        g_one = g_att[...] * ones[n]
        scores = mm_nt(k_all, q_one)
        probs = jnp.exp2(scores * LOG2E - logs[0, n : n + 1, :])
        g_probs = mm_nt(v_all, g_one)
        level = jnp.sum(inner[n * size : (n + 1) * size], axis=0, keepdims=True)
        g_scores = (probs * (g_probs - level)).astype(LOW)
        part_v = mm(probs.astype(LOW), g_one)
        part_k = mm(g_scores, q_one)
        g_v = part_v if g_v is None else g_v + part_v
        g_k = part_k if g_k is None else g_k + part_k
        g_q.append(mm(k_turned[n * size : (n + 1) * size], g_scores))
    query = jnp.transpose(jnp.concatenate(g_q, axis=0)).astype(LOW)
    value = g_v.astype(LOW)
    g_qkv[0] = query
    g_qkv[1] = g_k.astype(LOW)
    g_qkv[2] = value
    sums[0:1, :] = jnp.sum(query.astype(F32), axis=0, keepdims=True)
    sums[1:2, :] = jnp.sum(value.astype(F32), axis=0, keepdims=True)


def attend_back(sc, qkv, att, g_att, logs):
    rows, width = att.shape
    size = width // H
    pair = 2 * size
    pairs = width // pair
    tile = spec((rows, pair), lambda j, sc: (0, j))
    return call(
        functools.partial(attend_back_body, size ** (-0.5)),
        (pairs,),
        [
            tile,
            spec((rows, pair), lambda j, sc: (0, pairs + j)),
            spec((rows, pair), lambda j, sc: (0, 2 * pairs + j)),
            tile,
            tile,
            spec((1, 2, rows), lambda j, sc: (j, 0, 0)),
        ],
        [spec((3, rows, pair), lambda j, sc: (0, 0, j)), spec((2, pair), lambda j, sc: (0, j))],
        [shape((3, rows, width), LOW), shape((2, width), F32)],
    )(sc, qkv, qkv, qkv, att, g_att, logs)


def token_grads_body(sc, g_qkv, w, base, spots, spots_column, tokens_out, fill_out, total):
    rows = base.shape[0]
    width = base.shape[1]
    step = pl.program_id(0)
    grad = base[...]
    for n in range(3):
        grad = grad + mm_nt(g_qkv[n], w[:, n * width : (n + 1) * width])
    placed = one_hot_rows(sc, spots[...], step * rows, rows)
    kept = 1.0 - jnp.sum(placed, axis=1, keepdims=True)
    tokens_out[...] = (grad * kept).astype(LOW)
    slots = spots_column.shape[0]
    place = lax.broadcasted_iota(jnp.int32, (slots, rows), 1) + step * rows
    slot = lax.broadcasted_iota(jnp.int32, (slots, rows), 0)
    hit = (place == spots_column[...]) & (slot < sc[2])
    picked = mm(jnp.where(hit, 1.0, 0.0).astype(LOW), grad.astype(LOW))

    @pl.when(step == 0)
    def _():
        total[...] = picked

    @pl.when(step > 0)
    def _():
        total[...] += picked

    fill_out[...] = total[...].astype(LOW)


def token_grads(sc, g_qkv, w_qkv, base, spots, slots):
    rows, width = base.shape
    block = 128
    row = lambda i, sc: (i, 0)
    whole = lambda i, sc: (0, 0)
    tile = spec((block, width), row)
    return call(
        token_grads_body,
        (rows // block,),
        [
            spec((3, block, width), lambda i, sc: (0, i, 0)),
            spec(w_qkv.shape, whole),
            tile,
            spec(spots.shape, whole),
            spec((slots, 1), whole),
        ],
        [tile, spec((slots, width), whole)],
        [shape((rows, width), LOW), shape((slots, width), LOW)],
        scratch=[pltpu.VMEM((slots, width), F32)],
    )(sc, g_qkv, w_qkv, base, spots, spots.reshape(slots, 1))


def weight_body(counts, kinds, lefts, sc, *refs):
    used = 2 * (1 + max(lefts))
    left_refs, ins = refs[:used], refs[used : used + 2 * len(counts)]
    outs = list(refs[used + 2 * len(counts) :])
    slots = {}
    for kind, copies in (("halved", 2), ("whole", 1)):
        if kind in kinds:
            slots[kind], outs = outs[:copies], outs[copies:]
    step = pl.program_id(0)
    first = 0
    for n, (count, kind, at) in enumerate(zip(counts, kinds, lefts)):
        left, left_other = left_refs[2 * at : 2 * at + 2]
        mine, other = ins[2 * n], ins[2 * n + 1]

        def work(left=left, left_other=left_other, mine=mine, other=other, kind=kind):
            places, _, depth = left.shape
            rows_of = lambda ref: ref[...].reshape(-1, depth)
            total = mm(rows_of(left), mine[...]) + mm(rows_of(left_other), other[...])
            total = total.astype(LOW).reshape(places, -1, total.shape[-1])
            if kind == "whole":
                slots[kind][0][...] = total
            else:
                slots[kind][0][...] = total[: places // 2]
                slots[kind][1][...] = total[places // 2 :]

        if len(counts) == 1:
            work()
        else:
            pl.when((step >= first) & (step < first + count))(work)
        first += count


def weight_grad(sc, lefts, segments):
    places, chunk, depth = lefts[0][0].shape
    left_spec = spec((places, chunk, depth), lambda j, sc: (0, 0, 0))
    in_specs = [left_spec] * (2 * len(lefts))
    operands = [value for pair in lefts for value in pair]
    first = 0
    for mine, other, count, index, kind, matrix in segments:
        def at(j, sc, first=first, count=count, index=index):
            return index(jnp.clip(j - first, 0, count - 1), sc)

        block = (depth, WIDE) if mine.ndim == 2 else (None, depth, WIDE)
        in_specs += [spec(block, at), spec(block, at)]
        operands += [mine, other]
        first += count
    blocks = first
    out_specs, out_shapes = [], []
    done = 0
    for kind in ("halved", "whole"):
        count = sum(item[2] for item in segments if item[4] == kind)
        if count:
            kept = places if kind == "whole" else places // 2
            at = lambda j, sc, done=done, count=count: (jnp.clip(j - done, 0, count - 1), 0, 0, 0)
            copies = 1 if kind == "whole" else 2
            out_specs += [spec((None, kept, chunk, WIDE), at)] * copies
            out_shapes += [shape((count, kept, chunk, WIDE), LOW)] * copies
            done += count
    pick = lambda n: tuple(item[n] for item in segments)
    return call(
        functools.partial(weight_body, pick(2), pick(4), pick(5)),
        (blocks,),
        in_specs,
        out_specs,
        out_shapes,
    )(sc, *operands)


def add_body(count, sc, *refs):
    for n in range(count):
        keep, got = refs[2 * n], refs[2 * n + 1]
        left, sent = refs[2 * count + 2 * n], refs[2 * count + 2 * n + 1]
        total = (keep[...].astype(F32) + got[...].astype(F32)).astype(LOW)
        left[...] = total[:, :, 0]
        sent[...] = total[:, :, 1]


def add_halves(sc, items):
    tile = WIDE // 2
    in_specs, out_specs, out_shapes, operands = [], [], [], []
    for keep, got, dims in items:
        for value in (keep, got):
            operands.append(value.reshape(dims + (WIDE,)))
            in_specs.append(spec(dims + (tile,), lambda j, sc: (0, 0, 0, 0, j)))
        half = dims[:2] + dims[3:]
        out_specs += [spec(half + (tile,), lambda j, sc: (0, 0, 0, j))] * 2
        out_shapes += [shape(half + (WIDE,), LOW)] * 2
    found = call(functools.partial(add_body, len(items)), (WIDE // tile,), in_specs, out_specs, out_shapes, weight=1)(
        sc, *operands
    )
    return [(found[2 * n], found[2 * n + 1]) for n in range(len(items))]


def last_body(plan, sc, *refs):
    ins = len(plan) * 2
    places = {}
    for n, (blocks, targets) in enumerate(plan):
        keep, got = refs[2 * n], refs[2 * n + 1]
        for block, (target, turned) in zip(range(blocks), targets):
            out = refs[ins + target]
            at = places.get(target, 0)
            total = keep[block].astype(F32) + got[block].astype(F32)
            if turned:
                out[at : at + WIDE, :] = jnp.transpose(total)
            else:
                out[:, at : at + WIDE] = total
            places[target] = at + WIDE


def add_last(sc, items, outs):
    whole = lambda n: (lambda j, sc: (0,) * n)
    operands = [value for item in items for value in item[:2]]
    plan = tuple((item[0].shape[0], item[2]) for item in items)
    return call(
        functools.partial(last_body, plan),
        (1,),
        [spec(value.shape, whole(3)) for value in operands],
        [spec(dims, whole(2)) for dims in outs],
        [shape(dims, F32) for dims in outs],
        weight=1,
    )(sc, *operands)


def stack_body(sc, *refs):
    count = len(refs) - 2
    out, sems = refs[count], refs[count + 1]
    copies = [pltpu.make_async_copy(refs[n], out.at[n], sems.at[n]) for n in range(count)]
    for copy in copies:
        copy.start()
    for copy in copies:
        copy.wait()


def stack(sc, *values):
    anywhere = pl.BlockSpec(memory_space=pl.ANY)
    return call(
        stack_body,
        (1,),
        [anywhere] * len(values),
        anywhere,
        shape((len(values),) + values[0].shape, LOW),
        scratch=[pltpu.SemaphoreType.DMA((len(values),))],
        weight=1,
    )(sc, *values)


def swap(value, axis, bit):
    size = lax.axis_size(axis)
    return lax.ppermute(value, axis, [(n, n ^ bit) for n in range(size)])


def halves(value, bits, step):
    shards, blocks, places, chunk, wide = value.shape
    axis, bit = step
    if axis == "ffn":
        return value[: shards // 2], value[shards // 2 :], bits
    at = bits.index(bit)
    low = 1 << (len(bits) - 1 - at)
    parts = value.reshape(shards, blocks, places // (2 * low), 2, low, chunk, wide)
    dims = (shards, blocks, places // 2, chunk, wide)
    return (
        parts[:, :, :, 0].reshape(dims),
        parts[:, :, :, 1].reshape(dims),
        bits[:at] + bits[at + 1 :],
    )


class Line:
    def __init__(self):
        self.last = None

    def put(self, *values):
        if self.last is None:
            return values if len(values) > 1 else values[0]
        tied = lax.optimization_barrier(values + (self.last,))[:-1]
        return tied if len(values) > 1 else tied[0]

    def mark(self, value):
        self.last = value


class Stream:
    def __init__(self, line, bits, steps, whole=None, keep=None, send=None):
        self.line, self.bits, self.steps = line, list(bits), list(steps)
        if keep is None:
            keep, send, self.bits = halves(whole, self.bits, self.steps[0])
        elif self.steps[0][0] == "seq":
            self.bits.remove(self.steps[0][1])
        self.post(keep, send)

    def post(self, keep, send):
        self.keep = keep
        self.got = swap(send, *self.steps.pop(0))

    def advance(self):
        keep, got = self.line.put(self.keep, self.got)
        if self.steps:
            step = self.steps[0]
            keep_a, send_a, left = halves(keep, self.bits, step)
            keep_b, send_b, left = halves(got, self.bits, step)
            self.bits = left
            add = lambda a, b: (a.astype(F32) + b.astype(F32)).astype(LOW)
            send = add(send_a, send_b)
            keep = add(keep_a, keep_b)
            self.line.mark(keep)
            self.post(keep, send)
            return None
        total = keep.astype(F32) + got.astype(F32)
        self.line.mark(total)
        return total

    def finish(self):
        while True:
            total = self.advance()
            if total is not None:
                return total


class Streams:
    def __init__(self, sc, line, items):
        self.sc, self.line, self.items = sc, line, []
        for keep, send, bits, steps in items:
            axis, bit = steps[0]
            bits = [b for b in bits if axis != "seq" or b != bit]
            self.items.append([keep, swap(send, axis, bit), keep.shape, bits, list(steps[1:])])

    def advance(self):
        work = []
        tied = self.line.put(*[value for item in self.items for value in item[:2]])
        for n, (_, _, dims, bits, steps) in enumerate(self.items):
            shards, blocks, places, chunk, _ = dims
            axis, bit = steps[0]
            if axis == "ffn":
                split = (1, 1, 2, dims[0] // 2 * blocks * places * chunk)
                left = (shards // 2, blocks, places, chunk, WIDE)
            else:
                at = bits.index(bit)
                low = 1 << (len(bits) - 1 - at)
                split = (shards * blocks, places // (2 * low), 2, low * chunk)
                left = (shards, blocks, places // 2, chunk, WIDE)
                bits.remove(bit)
            work.append((tied[2 * n], tied[2 * n + 1], split, left))
        found = add_halves(self.sc, [item[:3] for item in work])
        self.line.mark(found[0][0])
        for n, (keep, send) in enumerate(found):
            left = work[n][3]
            axis, bit = self.items[n][4].pop(0)
            self.items[n][:3] = [keep.reshape(left), swap(send.reshape(left), axis, bit), left]

    def finish(self, targets, outs):
        tied = self.line.put(*[value for item in self.items for value in item[:2]])
        flat = lambda v: v.reshape((-1,) + v.shape[3:])
        items = [(flat(tied[2 * n]), flat(tied[2 * n + 1]), targets[n]) for n in range(len(self.items))]
        found = add_last(self.sc, items, outs)
        self.line.mark(found[0])
        return found


def all_sum(line, value, n_seq, n_ffn):
    for axis, size in (("seq", n_seq), ("ffn", n_ffn)):
        for bit in bits_of(size):
            value = value + line.put(swap(value, axis, bit))
            line.mark(value)
            yield value


def bits_of(size):
    found = []
    bit = 1
    while bit < size:
        found.append(bit)
        bit *= 2
    return found


def columns_of(found):
    found = found.reshape((-1,) + found.shape[3:])
    return jnp.transpose(found, (1, 0, 2)).reshape(found.shape[1], -1)


def on_device(
    tokens,
    spots,
    counts,
    fill,
    cot,
    w_qkv,
    b_q,
    b_v,
    w_out,
    b_out,
    gain_one,
    shift_one,
    w_up,
    b_up,
    w_down,
    b_down,
    gain_two,
    shift_two,
):
    n_seq, n_ffn = lax.axis_size("seq"), lax.axis_size("ffn")
    seq, ffn = lax.axis_index("seq"), lax.axis_index("ffn")
    rows, width = tokens.shape
    slots = spots.shape[1]
    units = w_up.shape[1]
    sc = jnp.stack([seq.astype(jnp.int32), ffn.astype(jnp.int32), counts[0]])
    fill, cot = fill[0], cot[0]
    vector = lambda v: v.astype(F32).reshape(1, -1)
    gain_a, shift_a, gain_b, shift_b = (vector(v) for v in (gain_one, shift_one, gain_two, shift_two))
    bias_qkv = vector(jnp.concatenate([b_q, jnp.zeros_like(b_q), b_v]))

    order = ffn ^ jnp.arange(n_ffn)
    line = Line()
    pairs = n_ffn == 2
    if pairs:
        split = "pairs"
        size = units // 8
        core, near = seq % 2, (seq // 2) % 4

        def cut(away):
            place = (near ^ away) * 2 + core
            up = lax.dynamic_slice(w_up, (0, place * size), (width, size))
            down = lax.dynamic_slice(w_down, (place * size, 0), (size, width))
            return up, down

        up_own, down_own = cut(0)
        up_own = swap(up_own, "ffn", 1)
        down_own = swap(down_own, "ffn", 1)
        b_other = swap(b_up, "ffn", 1)
    else:
        split = "stack"
        ups = (jnp.take(lax.all_gather(w_up, "ffn"), order[1:], axis=0),)
        downs = (jnp.take(lax.all_gather(w_down, "ffn"), order[1:], axis=0),)
        b_other = jnp.take(lax.all_gather(b_up, "ffn"), order[1:], axis=0)

    x, x_keep, x_send, qkv = embed_qkv(sc, tokens, spots, fill, w_qkv, bias_qkv, n_seq)
    line.mark(qkv)
    x_get = swap(x_send, "seq", 1)
    if pairs:
        up_own = line.put(up_own)
        up_y, up_z = swap(up_own, "seq", 2), swap(up_own, "seq", 4)
        up_far, down_far = cut(3)
        up_far = swap(line.put(up_far), "ffn", 1)
        down_far = swap(line.put(down_far), "ffn", 1)
    att, att_keep, att_send, logs = attend(sc, line.put(qkv), n_seq)
    line.mark(att)
    att_get = swap(att_send, "seq", 1)
    if pairs:
        up_near = stack(sc, *line.put(up_own, up_y, up_z))
        line.mark(up_near)
        up_near_other = swap(up_near, "seq", 1)
        down_own = line.put(down_own)
        down_y, down_z = swap(down_own, "seq", 2), swap(down_own, "seq", 4)
    hat, inv, low, n_keep, n_send = norm_one(sc, line.put(att), w_out, x, vector(b_out), gain_a, shift_a, n_seq)
    line.mark(low)
    n_get = swap(n_send, "seq", 1)
    hid_own, slope_own, total = ffn_fwd(sc, line.put(low), vector(b_up), (w_up,), (w_down,), "own")
    line.mark(hid_own)
    hid_own_get = swap(hid_own, "seq", 1)
    if pairs:
        down_near = stack(sc, *line.put(down_own, down_y, down_z))
        line.mark(down_near)
        down_near_other = swap(down_near, "seq", 1)
        up_far = line.put(up_far)[None]
        up_far_other = swap(up_far, "seq", 1)
        down_far = line.put(down_far)[None]
        down_far_other = swap(down_far, "seq", 1)
        ups = (up_near, up_near_other, up_far, up_far_other)
        downs = (down_near, down_near_other, down_far, down_far_other)
    hid_oth, slope_oth, total = ffn_fwd(sc, line.put(low), vector(b_other), ups, downs, split, total)
    line.mark(hid_oth)
    hid_oth_get = swap(hid_oth, "seq", 1)

    output, g_two, g_down, d_keep, d_send, sums_two = norm_two(
        sc, line.put(total), hat, gain_a, shift_a, vector(b_down), gain_b, shift_b, spots, cot, n_seq
    )
    line.mark(g_down)
    d_get = swap(d_send, "seq", 1)

    found_bits = bits_of(n_seq)
    seq_bits = [2] + found_bits[2:][::-1]
    ffn_steps = [("ffn", b) for b in bits_of(n_ffn)[::-1]]
    z_steps = [("seq", b) for b in found_bits[2:]]
    y_step = [("seq", 2)]
    x_first = ffn_steps + z_steps + y_step
    y_first = y_step + z_steps + ffn_steps
    per = units // WIDE
    half = per // 2
    shards = lambda v, n: v.reshape((n, -1) + v.shape[1:])
    column = lambda start: (lambda b, sc: (0, start + b))

    def big_first(left, oth, oth_get):
        mine, right = left
        (send,) = weight_grad(sc, [(line.put(mine), right)], [(oth, oth_get, half, column(0), "whole", 0)])
        line.mark(send)
        return shards(send, 1)

    def big_rest(left, own, own_get, oth, oth_get, send):
        mine, right = left
        keep_b, send_b, keep = weight_grad(
            sc, [(line.put(mine), right)],
            [
                (own, own_get, per - half, column(half), "halved", 0),
                (oth, oth_get, per - half, column(half), "halved", 0),
                (own, own_get, half, column(0), "whole", 0),
            ],
        )
        line.mark(keep)
        return Streams(sc, line, [
            (shards(keep, 1), send, seq_bits, x_first),
            (shards(keep_b, 2), shards(send_b, 2), seq_bits, y_first),
        ])

    def big_whole(left, own, own_get, oth, oth_get):
        n_oth = oth.shape[1] // WIDE
        mine, right = left
        (whole,) = weight_grad(
            sc, [(line.put(mine), right)],
            [(own, own_get, per, column(0), "whole", 0), (oth, oth_get, n_oth, column(0), "whole", 0)],
        )
        line.mark(whole)
        return Stream(line, seq_bits, x_first, whole=shards(whole, n_ffn))

    d_left, n_left = (d_keep, d_get), (n_keep, n_get)
    if pairs:
        d_first = big_first(d_left, hid_oth, hid_oth_get)
        downs_sum = big_rest(d_left, hid_own, hid_own_get, hid_oth, hid_oth_get, d_first)
    else:
        down_a = big_whole(d_left, hid_own, hid_own_get, hid_oth, hid_oth_get)

    gp_oth, bs_oth, g_total = ffn_bwd(sc, line.put(g_down), slope_oth, ups, downs, split)
    line.mark(gp_oth)
    gp_oth_get = swap(gp_oth, "seq", 1)
    gp_own, bs_own, g_total = ffn_bwd(sc, line.put(g_down), slope_own, (w_up,), (w_down,), "own", g_total)
    line.mark(gp_own)
    gp_own_get = swap(gp_own, "seq", 1)

    if pairs:
        downs_sum.advance()
        u_first = big_first(n_left, gp_oth, gp_oth_get)
        ups_sum = big_rest(n_left, gp_own, gp_own_get, gp_oth, gp_oth_get, u_first)
    else:
        up_a = big_whole(n_left, gp_own, gp_own_get, gp_oth, gp_oth_get)
    b_up_sums = jnp.concatenate([bs_own.reshape(1, units), bs_oth.reshape(n_ffn - 1, units)])
    b_up_sums = jnp.take(b_up_sums, order, axis=0).reshape(-1)

    g_one, g_att_low, g_att, sums_one = norm_one_back(sc, line.put(g_two), g_total, hat, inv, gain_a, w_out)
    line.mark(g_att)
    g_att_get = swap(g_att_low, "seq", 1)
    if pairs:
        downs_sum.advance()

    def narrow(mine, other, first, count, kind, matrix):
        per_row = mine.shape[-1] // WIDE
        blocks = per_row * (mine.shape[0] if mine.ndim == 3 else 1)
        each = blocks // n_ffn

        def index(b, sc):
            block = ((b // count) ^ sc[1]) * each + first + b % count
            return (0, block) if mine.ndim == 2 else (block // per_row, 0, block % per_row)

        return (mine, other, n_ffn * count, index, kind, matrix)

    def narrow_whole(left, mine, other):
        per_row = mine.shape[-1] // WIDE
        blocks = per_row * (mine.shape[0] if mine.ndim == 3 else 1)
        index = (lambda b, sc: (0, b)) if mine.ndim == 2 else (lambda b, sc: (b // per_row, 0, b % per_row))
        (whole,) = weight_grad(sc, [(line.put(left[0]), left[1])], [(mine, other, blocks, index, "whole", 0)])
        line.mark(whole)
        places, chunk = whole.shape[1:3]
        share = blocks * WIDE // n_ffn
        whole = jnp.transpose(whole, (1, 2, 0, 3)).reshape(places, chunk, n_ffn, share)
        whole = jnp.take(jnp.transpose(whole, (2, 0, 1, 3)), order, axis=0)[:, None]
        return Stream(line, seq_bits, x_first, whole=whole)

    g_qkv, sums_att = attend_back(sc, line.put(qkv), att, g_att, logs)
    line.mark(g_qkv)
    g_qkv_get = swap(g_qkv, "seq", 1)
    sums = jnp.concatenate([sums_two[:3].reshape(-1), sums_one[:3].reshape(-1), b_up_sums, sums_att.reshape(-1)])
    summing = all_sum(line, sums, n_seq, n_ffn)
    if pairs:
        ups_sum.advance()
        downs_sum.advance()
    grad_tokens, grad_fill = token_grads(sc, line.put(g_qkv), w_qkv, g_one, spots, slots)
    line.mark(grad_tokens)
    chunk = width // n_seq
    if pairs:
        keep_b, send_b, both = weight_grad(
            sc, [(line.put(x_keep), x_get), (att_keep, att_get)],
            [
                narrow(g_qkv, g_qkv_get, 2, 1, "halved", 0),
                narrow(g_att_low, g_att_get, 0, 1, "halved", 1),
                narrow(g_qkv, g_qkv_get, 0, 2, "whole", 0),
            ],
        )
        line.mark(keep_b)
        both = shards(both, 2)
        joint = lambda v: shards(v, 2).reshape(2, 2, 1, *v.shape[1:])
        by_shard = lambda v: jnp.swapaxes(joint(v), 0, 1).reshape(2, 2, *v.shape[1:])
        tail = Streams(sc, line, [
            (both[:1], both[1:], seq_bits, ffn_steps + y_step + z_steps),
            (by_shard(keep_b), by_shard(send_b), seq_bits, y_step + ffn_steps + z_steps),
        ])
        ups_sum.advance()
        (grad_down,) = downs_sum.finish([((0, True),) * 2] * 2, [(units, chunk)])
        next(summing)
        ups_sum.advance()
        next(summing)
        tail.advance()
        next(summing)
        (grad_up,) = ups_sum.finish([((0, False),) * 2] * 2, [(chunk, units)])
        next(summing)
        tail.advance()
        (*_, total_sums) = summing
        tail.advance()
        grad_qkv, grad_out = tail.finish(
            [((0, False), (0, False)), ((0, False), (1, False))], [(chunk, 3 * WIDE), (chunk, WIDE)]
        )
    else:
        out = narrow_whole((att_keep, att_get), g_att_low, g_att_get)
        qkv_a = narrow_whole((x_keep, x_get), g_qkv, g_qkv_get)
        (*_, total_sums) = summing
        grad_down, grad_up = columns_of(down_a.finish()).T, columns_of(up_a.finish())
        grad_out, grad_qkv = columns_of(out.finish()), columns_of(qkv_a.finish())

    part = lambda v, n: v[n * width : (n + 1) * width]
    return (
        output,
        grad_tokens,
        grad_fill[None],
        grad_qkv,
        total_sums[-2 * width : -width],
        total_sums[-width:],
        grad_out,
        part(total_sums, 5),
        part(total_sums, 3),
        part(total_sums, 4),
        grad_up,
        total_sums[6 * width : -2 * width],
        grad_down,
        part(total_sums, 2),
        part(total_sums, 0),
        part(total_sums, 1),
    )


def solution(mesh):
    rows = ("seq", "ffn")
    in_specs = (
        P(rows, None),
        P(rows, None),
        P(rows),
        P(rows, None, None),
        P(rows, None, None),
        P(),
        P(),
        P(),
        P(),
        P(),
        P(),
        P(),
        P(None, "ffn"),
        P("ffn"),
        P("ffn", None),
        P(),
        P(),
        P(),
    )
    out_specs = (
        P(rows, None),
        P(rows, None),
        P(rows, None, None),
        P("seq", "ffn"),
        P(),
        P(),
        P("seq", "ffn"),
        P(),
        P(),
        P(),
        P("seq", "ffn"),
        P(),
        P("ffn", "seq"),
        P(),
        P(),
        P(),
    )
    return jax.shard_map(on_device, mesh=mesh, in_specs=in_specs, out_specs=out_specs, check_vma=False)
```

time: 714 us -> 345 us (0.48); the launches traced: 705 us -> 344 us
  waiting for transfers between devices: 434 us -> 83.8 us
  Pallas kernels: 0 us -> 180 us
  matrix products: 159 us -> 0 us
  blocking collectives: 47.2 us -> 0 us
  starting transfers between devices: 0.57 us -> 43.8 us
  other arithmetic: 35.4 us -> 1.61 us
  local copies, waits for them, and re-layouts: 13.3 us -> 32 us
  between operations: 15.6 us -> 2.19 us
    reduce_scatter x8 -> x0, waiting for transfers between devices: 298 us -> none  [the longest x1 108 us: on_device(): lax.psum_scatter(grad_w_up.astype(jnp.bfloat16), 'seq', scatter_dimension...]
    pallas_call x0 -> x30, Pallas kernels: none -> 180 us  [the longest x5 36.8 us: weight_grad(): call(functools.partial(weight_body, pick(2), pick(4), pick(5)), (blocks,)...]
    dot_general x21 -> x0, matrix products: 159 us -> none  [the longest x4 46.8 us: dot_plain(): return jnp.dot(left, right, preferred_element_type=jnp.float32)]
    all_gather x2 -> x0, waiting for transfers between devices: 134 us -> none  [the longest x1 77.7 us: on_device(): lax.all_gather(w_down, 'ffn', axis=0, tiled=True)]
    ppermute x0 -> x52, waiting for transfers between devices: none -> 83.8 us  [swap(): return lax.ppermute(value, axis, [(n, n ^ bit) for n in range(size)])]
    ppermute x0 -> x52, starting transfers between devices: none -> 43.8 us  [swap(): return lax.ppermute(value, axis, [(n, n ^ bit) for n in range(size)])]
    psum x1 -> x0, blocking collectives: 42.2 us -> none  [on_device(): lax.psum((grad_b_q, grad_b_v, grad_b_out, grad_gain_one, grad_shift_one,...]
    convert_element_type x14 -> x1, other arithmetic: 19.1 us -> 0.02 us  [on_device(): vector = lambda v: v.astype(F32).reshape(1, -1)]
  transfers between devices with their start and end apart: 10 -> 52, of which waited for: 9 -> 18; matrix products, arithmetic and copies ran while one was open for 22% -> 3% of each run, Pallas kernels for 0% -> 49%
where the time goes in v1:
time: 345 us; the launch traced here: 344 us
  Pallas kernels  180 us (52%)
  waiting for transfers between devices  83.8 us (24%)
  starting transfers between devices  43.8 us (13%)
  local copies, waits for them, and re-layouts  32 us (9%)
    ppermute x52, waiting for transfers between devices, swap(): return lax.ppermute(value, axis, [(n, n ^ bit) for n in range(size)])  83.8 us
    ppermute x52, starting transfers between devices, swap(): return lax.ppermute(value, axis, [(n, n ^ bit) for n in range(size)])  43.8 us
    pallas_call x5, Pallas kernels, weight_grad(): call(functools.partial(weight_body, pick(2), pick(4), pick(5)), (blocks,)...  36.8 us
    pallas_call x2, Pallas kernels, ffn_fwd(): call(functools.partial(ffn_fwd_body, split, size, len(ups), first), (unit...  24.2 us
    unnamed x135, local copies, waits for them, and re-layouts  23.5 us
    pallas_call x2, Pallas kernels, ffn_bwd(): call(functools.partial(ffn_bwd_body, split, size, len(ups), first), (unit...  19.3 us
    pallas_call x1, Pallas kernels, attend_back(): call(functools.partial(attend_back_body, size ** (-0.5)), (pairs,), [tile...  16.4 us
    pallas_call x9, Pallas kernels, add_halves(): call(functools.partial(add_body, len(items)), (WIDE // tile,), in_specs,...  16.3 us
  transfers between devices with their start and end apart: 52, of which 18 were waited for; matrix products, arithmetic and copies ran while one was open for 3% of the time, Pallas kernels for 49%

profile of v1, /device:TPU:0, one launch (start us, length us, event | category | flops | bytes accessed | tf_op | source)
XLA Modules:
  0.0 343.6 jit_solution(4761485499019167161)
XLA Ops:
  2.9 2.9 collective-permute-start
  6.7 9.9 %shard_map.297 = (bf16[512,1024]{1,0:T(8,128)(2,1)S(1)}, bf16[8,64,512]{2,1,0:T(8,128)(2,1)S(1)}, bf16[8,64,512]{2,1,0:T(8,128)(2,1)}, bf16[512,3072]{1,0:T(8,128)(2,1)}) custom-call(s32[3]{0:T(128)S(1)} %pad_add_fusion.sc, bf16[512,1024]{1,0:T(8,128)(2,1)S(1)} %copy-done.20, s32[1,128]{1,0:T(1,128)S(1)} %copy-done.26, bf16[128,1024]{1,0:T(8,128)(2,1)S(1)} %bitcast.142, ...), custom_call_target="tpu_custom_call" | custom-call | flops 1 | bytes 1 | tf_op jit(solution)/shard_map/pallas_call | solution.py:99
  26.6 12.2 %shard_map.298 = (bf16[512,1024]{1,0:T(8,128)(2,1)S(1)}, bf16[8,64,512]{2,1,0:T(8,128)(2,1)S(1)}, bf16[8,64,512]{2,1,0:T(8,128)(2,1)}, f32[8,2,512]{2,1,0:T(2,128)S(1)}) custom-call(s32[3]{0:T(128)S(1)} %pad_add_fusion.sc, bf16[512,3072]{1,0:T(8,128)(2,1)S(1)} %copy-done, bf16[512,3072]{1,0:T(8,128)(2,1)S(1)} %copy-done, bf16[512,3072]{1,0:T(8,128)(2,1)S(1)} %copy-done), custom_call_target="tpu_custom_call" | custom-call | flops 1 | bytes 1 | tf_op jit(solution)/shard_map/pallas_call | solution.py:156
  40.7 9.3 %shard_map.300 = (f32[512,1024]{1,0:T(8,128)}, f32[512,1]{1,0:T(8,128)S(1)}, bf16[512,1024]{1,0:T(8,128)(2,1)S(1)}, bf16[8,64,512]{2,1,0:T(8,128)(2,1)S(1)}, bf16[8,64,512]{2,1,0:T(8,128)(2,1)S(1)}) custom-call(s32[3]{0:T(128)S(1)} %pad_add_fusion.sc, bf16[512,1024]{1,0:T(8,128)(2,1)S(1)} %get-tuple-element.189.att, bf16[1024,1024]{1,0:T(8,128)(2,1)} %w.6, ...), custom_call_target="tpu_custom_call" | custom-call | flops 1 | bytes 1 | tf_op jit(solution)/shard_map/pallas_call | solution.py:200
  50.0 11.7 %shard_map.301 = (bf16[512,2048]{1,0:T(8,128)(2,1)S(1)}, bf16[512,2048]{1,0:T(8,128)(2,1)S(1)}, f32[512,1024]{1,0:T(8,128)}) custom-call(s32[3]{0:T(128)S(1)} %pad_add_fusion.sc, bf16[512,1024]{1,0:T(8,128)(2,1)S(1)} %get-tuple-element.198.refs_0_, f32[1,2048]{1,0:T(1,128)S(1)} %bitcast.147, bf16[1024,2048]{1,0:T(8,128)(2,1)} %refs_2_.3, ...), custom_call_target="tpu_custom_call" | custom-call | flops 1 | bytes 1 | tf_op jit(solution)/shard_map/pallas_call | solution.py:307
  65.5 12.7 %collective-permute-done.11 = bf16[256,1024]{1,0:T(8,128)(2,1)S(1)} collective-permute-done((bf16[256,1024]{1,0:T(8,128)(2,1)S(1)}, bf16[256,1024]{1,0:T(8,128)(2,1)S(1)}, u32[]{:S(2)}, u32[]{:S(2)}) %collective-permute-start.11) | collective-permute-done | bytes 524320 | tf_op jit(solution)/shard_map/ppermute | solution.py:704
  78.2 10.5 %collective-permute-done.8 = bf16[1024,256]{1,0:T(8,128)(2,1)S(1)} collective-permute-done((bf16[1024,256]{1,0:T(8,128)(2,1)S(1)}, bf16[1024,256]{1,0:T(8,128)(2,1)S(1)}, u32[]{:S(2)}, u32[]{:S(2)}) %collective-permute-start.8) | collective-permute-done | bytes 524320 | tf_op jit(solution)/shard_map/ppermute | solution.py:704
  89.1 3.3 collective-permute-done.6
  94.1 12.5 %shard_map.303 = (bf16[512,2048]{1,0:T(8,128)(2,1)}, bf16[512,2048]{1,0:T(8,128)(2,1)}, f32[512,1024]{1,0:T(8,128)}) custom-call(s32[3]{0:T(128)S(1)} %pad_add_fusion.sc, bf16[512,1024]{1,0:T(8,128)(2,1)S(1)} %get-tuple-element.198.refs_0_, f32[1,2048]{1,0:T(1,128)S(1)} %bitcast.146, bf16[3,1024,256]{2,1,0:T(8,128)(2,1)S(1)} %shard_map.299.refs_2_, ...), custom_call_target="tpu_custom_call" | custom-call | flops 1 | bytes 1 | tf_op jit(solution)/shard_map/pallas_call | solution.py:307
  107.2 8.6 %shard_map.304 = (bf16[512,1024]{1,0:T(8,128)(2,1)}, f32[512,1024]{1,0:T(8,128)S(1)}, bf16[512,1024]{1,0:T(8,128)(2,1)S(1)}, bf16[8,64,512]{2,1,0:T(8,128)(2,1)S...) custom-call(s32[3]{0:T(128)S(1)} %pad_add_fusion.sc, f32[512,1024]{1,0:T(8,128)} %get-tuple-element.206.mixed, ...), custom_call_target="tpu_custom_call" | custom-call | flops 99999997952 | bytes 1 | tf_op jit(solution)/shard_map/pallas_call | solution.py:404
  120.2 3.9 %shard_map.305 = bf16[2,8,64,512]{3,2,1,0:T(8,128)(2,1)} custom-call(s32[3]{0:T(128)S(1)} %pad_add_fusion.sc, bf16[8,64,512]{2,1,0:T(8,128)(2,1)S(1)} %get-tuple-element.213.refs_0_, bf16[8,64,512]{2,1,0:T(8,128)(2,1)S(1)} %collective-permute-done.13.refs_1_, bf16[512,2048]{1,0:T(8,128)(2,1)S(1)} %copy-done.2, bf16[512,2048]{1,0:T(8,128)(2,1)} %copy-done.47), custom_call_target="tpu_custom_call" | custom-call | flops 1 | bytes 1 | tf_op jit(solution)/shard_map/pallas_call | solution.py:615
  124.1 8.7 %shard_map.306 = (bf16[4,4,64,512]{3,2,1,0:T(8,128)(2,1)S(1)}, bf16[4,4,64,512]{3,2,1,0:T(8,128)(2,1)}, bf16[2,8,64,512]{3,2,1,0:T(8,128)(2,1)S(1)}) custom-call(s32[3]{0:T(128)S(1)} %pad_add_fusion.sc, bf16[8,64,512]{2,1,0:T(8,128)(2,1)S(1)} %get-tuple-element.213.refs_0_, bf16[8,64,512]{2,1,0:T(8,128)(2,1)S(1)} %collective-permute-done.13.refs_1_, ...), custom_call_target="tpu_custom_call" | custom-call | flops 1 | bytes 1 | tf_op jit(solution)/shard_map/pallas_call | solution.py:615
  141.9 9.7 %shard_map.307 = (bf16[512,2048]{1,0:T(8,128)(2,1)}, f32[1,2048]{1,0:T(1,128)S(1)}, f32[512,1024]{1,0:T(8,128)}) custom-call(s32[3]{0:T(128)S(1)} %pad_add_fusion.sc, bf16[512,1024]{1,0:T(8,128)(2,1)S(1)} %get-tuple-element.220.refs_0_, bf16[512,2048]{1,0:T(8,128)(2,1)} %get-tuple-element.218.refs_1_, bf16[3,1024,256]{2,1,0:T(8,128)(2,1)S(1)} %shard_map.299.refs_2_, ...), custom_call_target="tpu_custom_call" | custom-call | flops 1 | bytes 1 | tf_op jit(solution)/shard_map/pallas_call | solution.py:353
  152.1 9.5 %shard_map.308 = (bf16[512,2048]{1,0:T(8,128)(2,1)}, f32[1,2048]{1,0:T(1,128)S(1)}, f32[512,1024]{1,0:T(8,128)S(1)}) custom-call(s32[3]{0:T(128)S(1)} %pad_add_fusion.sc, bf16[512,1024]{1,0:T(8,128)(2,1)S(1)} %get-tuple-element.220.refs_0_, bf16[512,2048]{1,0:T(8,128)(2,1)} %copy-done.16, bf16[1024,2048]{1,0:T(8,128)(2,1)} %refs_2_.3, ...), custom_call_target="tpu_custom_call" | custom-call | flops 1 | bytes 1 | tf_op jit(solution)/shard_map/pallas_call | solution.py:353
  163.0 3.4 shard_map.309
  171.9 4.1 %shard_map.310 = bf16[2,8,64,512]{3,2,1,0:T(8,128)(2,1)} custom-call(s32[3]{0:T(128)S(1)} %pad_add_fusion.sc, bf16[8,64,512]{2,1,0:T(8,128)(2,1)S(1)} %copy-done.19, bf16[8,64,512]{2,1,0:T(8,128)(2,1)} %collective-permute-done.20.refs_1_, bf16[512,2048]{1,0:T(8,128)(2,1)S(1)} %copy-done.1, bf16[512,2048]{1,0:T(8,128)(2,1)} %collective-permute-done.21.refs_3_.refs_5_), custom_call_target="tpu_custom_call" | custom-call | flops 1 | bytes 1 | tf_op jit(solution)/shard_map/pallas_call | solution.py:615
  176.0 9.0 %shard_map.311 = (bf16[4,4,64,512]{3,2,1,0:T(8,128)(2,1)S(1)}, bf16[4,4,64,512]{3,2,1,0:T(8,128)(2,1)}, bf16[2,8,64,512]{3,2,1,0:T(8,128)(2,1)S(1)}) custom-call(s32[3]{0:T(128)S(1)} %pad_add_fusion.sc, bf16[8,64,512]{2,1,0:T(8,128)(2,1)S(1)} %copy-done.19, bf16[8,64,512]{2,1,0:T(8,128)(2,1)} %collective-permute-done.20.refs_1_, ...), custom_call_target="tpu_custom_call" | custom-call | flops 1 | bytes 1 | tf_op jit(solution)/shard_map/pallas_call | solution.py:615
  185.0 8.0 %shard_map.312 = (f32[512,1024]{1,0:T(8,128)S(1)}, bf16[512,1024]{1,0:T(8,128)(2,1)S(1)}, bf16[512,1024]{1,0:T(8,128)(2,1)S(1)}, f32[8,1024]{1,0:T(8,128)S(1)}) custom-call(s32[3]{0:T(128)S(1)} %pad_add_fusion.sc, f32[512,1024]{1,0:T(8,128)} %copy-done.15, f32[512,1024]{1,0:T(8,128)} %copy-done.17, f32[512,1024]{1,0:T(8,128)} %get-tuple-element.207.hat_one.hat, ...), custom_call_target="tpu_custom_call" | custom-call | flops 1 | bytes 1 | tf_op jit(solution)/shard_map/pallas_call | solution.py:444
  195.9 2.6 shard_map.313
  200.6 2.6 collective-permute-start.23
  203.2 16.4 %shard_map.314 = (bf16[3,512,1024]{2,1,0:T(8,128)(2,1)}, f32[2,1024]{1,0:T(2,128)S(1)}) custom-call(s32[3]{0:T(128)S(1)} %pad_add_fusion.sc, bf16[512,3072]{1,0:T(8,128)(2,1)} %get-tuple-element.247.q.k.v, bf16[512,3072]{1,0:T(8,128)(2,1)} %get-tuple-element.247.q.k.v, bf16[512,3072]{1,0:T(8,128)(2,1)} %get-tuple-element.247.q.k.v, ...), custom_call_target="tpu_custom_call" | custom-call | flops 1 | bytes 1 | tf_op jit(solution)/shard_map/pallas_call | solution.py:491
  224.3 2.5 shard_map.315
  227.3 8.0 %collective-permute-done.24 = bf16[2,2,1,64,512]{4,3,1,0,2:T(8,128)(2,1)S(1)} collective-permute-done((bf16[2,2,1,64,512]{4,3,1,0,2:T(8,128)(2,1)}, bf16[2,2,1,64,512]{4,3,1,0,2:T(8,128)(2,1)S(1)}, u32[]{:S(2)}, u32[]{:S(2)}) %collective-permute-start.24) | collective-permute-done | bytes 262176 | tf_op jit(solution)/shard_map/ppermute | solution.py:704
  239.0 14.3 %shard_map.317 = (bf16[512,1024]{1,0:T(8,128)(2,1)}, bf16[128,1024]{1,0:T(8,128)(2,1)}) custom-call(s32[3]{0:T(128)S(1)} %pad_add_fusion.sc, bf16[3,512,1024]{2,1,0:T(8,128)(2,1)} %get-tuple-element.265.g_qkv.refs_4_.refs_8_, bf16[1024,3072]{1,0:T(8,128)(2,1)} %w.7, f32[512,1024]{1,0:T(8,128)S(1)} %get-tuple-element.266.base, s32[1,128]{1,0:T(1,128)S(1)} %copy-done.27, ...), custom_call_target="tpu_custom_call" | custom-call | flops 1 | bytes 1 | tf_op jit(solution)/shard_map/pallas_call | solution.py:540
  255.6 11.2 %shard_map.318 = (bf16[4,4,64,512]{3,2,1,0:T(8,128)(2,1)S(1)}, bf16[4,4,64,512]{3,2,1,0:T(8,128)(2,1)S(1)}, bf16[4,8,64,512]{3,2,1,0:T(8,128)(2,1)}) custom-call(s32[3]{0:T(128)S(1)} %pad_add_fusion.sc, bf16[8,64,512]{2,1,0:T(8,128)(2,1)S(1)} %copy-done.22, bf16[8,64,512]{2,1,0:T(8,128)(2,1)} %collective-permute-done.27.refs_1_, ...), custom_call_target="tpu_custom_call" | custom-call | flops 1 | bytes 1 | tf_op jit(solution)/shard_map/pallas_call | solution.py:615
  269.6 2.9 collective-permute-start.40
  276.6 12.8 %collective-permute-done.39 = bf16[1,2,2,64,512]{4,3,2,1,0:T(8,128)(2,1)S(1)} collective-permute-done((bf16[1,2,2,64,512]{4,3,2,1,0:T(8,128)(2,1)S(1)}, bf16[1,2,2,64,512]{4,3,2,1,0:T(8,128)(2,1)S(1)}, u32[]{:S(2)}, u32[]{:S(2)}) %collective-permute-start.39) | collective-permute-done | bytes 262176 | tf_op jit(solution)/shard_map/ppermute | solution.py:704
  289.4 5.5 %collective-permute-done.40 = bf16[2,2,1,64,512]{4,3,1,0,2:T(8,128)(2,1)S(1)} collective-permute-done((bf16[2,2,1,64,512]{4,3,1,0,2:T(8,128)(2,1)S(1)}, bf16[2,2,1,64,512]{4,3,1,0,2:T(8,128)(2,1)S(1)}, u32[]{:S(2)}, u32[]{:S(2)}) %collective-permute-start.40) | collective-permute-done | bytes 262176 | tf_op jit(solution)/shard_map/ppermute | solution.py:704
  308.2 8.0 %collective-permute-done.41 = bf16[1,2,4,64,512]{4,3,2,1,0:T(8,128)(2,1)S(1)} collective-permute-done((bf16[1,2,4,64,512]{4,3,2,1,0:T(8,128)(2,1)S(1)}, bf16[1,2,4,64,512]{4,3,2,1,0:T(8,128)(2,1)S(1)}, u32[]{:S(2)}, u32[]{:S(2)}) %collective-permute-start.41) | collective-permute-done | bytes 524320 | tf_op jit(solution)/shard_map/ppermute | solution.py:704
  322.4 2.4 collective-permute-done.49
  327.3 2.8 collective-permute-done.48
  334.6 6.2 %collective-permute-done.50 = bf16[1,2,1,64,512]{4,3,1,2,0:T(8,128)(2,1)S(1)} collective-permute-done((bf16[1,2,1,64,512]{4,3,1,2,0:T(8,128)(2,1)S(1)}, bf16[1,2,1,64,512]{4,3,1,2,0:T(8,128)(2,1)S(1)}, u32[]{:S(2)}, u32[]{:S(2)}) %collective-permute-start.50) | collective-permute-done | bytes 131104 | tf_op jit(solution)/shard_map/ppermute | solution.py:704
  (275 shorter events, 93.3 us)
Async XLA Ops:
  2.9 14.9 %collective-permute-start = (bf16[1024,256]{1,0:T(8,128)(2,1)S(1)}, bf16[1024,256]{1,0:T(8,128)(2,1)S(1)}, u32[]{:S(2)}, u32[]{:S(2)}) collective-permute-start(bf16[1024,256]{1,0:T(8,128)(2,1)S(1)} %get-tuple-element.367), channel_id=1, source_target_pairs={{0,1},{1,0},{2,3},{3,2},{4,5},{5,4},{6,7},{7,6},{8,9},{9,8},{10,11... | collective-permute-start | bytes 1572872 | tf_op jit(solution)/shard_map/ppermute | solution.py:704
  17.8 21.0 %collective-permute-start.1 = (bf16[1024,256]{1,0:T(8,128)(2,1)S(1)}, bf16[1024,256]{1,0:T(8,128)(2,1)S(1)}, u32[]{:S(2)}, u32[]{:S(2)}) collective-permute-start(bf16[1024,256]{1,0:T(8,128)(2,1)S(1)} %collective-permute-done.refs_0_), channel_id=1, source_target_pairs={{0,4},{2,6},{4,0},{6,2},{8,12},{10,14},{12,8},{14,10},{16,20},{18,... | collective-permute-start | bytes 1572872 | tf_op jit(solution)/shard_map/ppermute | solution.py:704
  19.5 19.2 %collective-permute-start.2 = (bf16[1024,256]{1,0:T(8,128)(2,1)S(1)}, bf16[1024,256]{1,0:T(8,128)(2,1)S(1)}, u32[]{:S(2)}, u32[]{:S(2)}) collective-permute-start(bf16[1024,256]{1,0:T(8,128)(2,1)S(1)} %collective-permute-done.refs_0_), channel_id=1, source_target_pairs={{0,8},{2,10},{4,12},{6,14},{8,0},{10,2},{12,4},{14,6},{16,24},{18,... | collective-permute-start | bytes 1572872 | tf_op jit(solution)/shard_map/ppermute | solution.py:704
  23.2 16.4 %collective-permute-start.3 = (bf16[256,1024]{1,0:T(8,128)(2,1)S(1)}, bf16[256,1024]{1,0:T(8,128)(2,1)S(1)}, u32[]{:S(2)}, u32[]{:S(2)}) collective-permute-start(bf16[256,1024]{1,0:T(8,128)(2,1)S(1)} %get-tuple-element.365), channel_id=1, source_target_pairs={{0,1},{1,0},{2,3},{3,2},{4,5},{5,4},{6,7},{7,6},{8,9},{9,8},{10,11... | collective-permute-start | bytes 1572872 | tf_op jit(solution)/shard_map/ppermute | solution.py:704
  39.6 22.2 %collective-permute-start.4 = (bf16[256,1024]{1,0:T(8,128)(2,1)S(1)}, bf16[256,1024]{1,0:T(8,128)(2,1)S(1)}, u32[]{:S(2)}, u32[]{:S(2)}) collective-permute-start(bf16[256,1024]{1,0:T(8,128)(2,1)S(1)} %collective-permute-done.3.refs_0_), channel_id=1, source_target_pairs={{0,4},{2,6},{4,0},{6,2},{8,12},{10,14},{12,8},{14,10},{16,20},{18,... | collective-permute-start | bytes 1572872 | tf_op jit(solution)/shard_map/ppermute | solution.py:704
  40.1 21.6 %collective-permute-start.5 = (bf16[256,1024]{1,0:T(8,128)(2,1)S(1)}, bf16[256,1024]{1,0:T(8,128)(2,1)S(1)}, u32[]{:S(2)}, u32[]{:S(2)}) collective-permute-start(bf16[256,1024]{1,0:T(8,128)(2,1)S(1)} %collective-permute-done.3.refs_0_), channel_id=1, source_target_pairs={{0,8},{2,10},{4,12},{6,14},{8,0},{10,2},{12,4},{14,6},{16,24},{18,... | collective-permute-start | bytes 1572872 | tf_op jit(solution)/shard_map/ppermute | solution.py:704
  40.6 51.8 %collective-permute-start.7 = (bf16[3,1024,256]{2,1,0:T(8,128)(2,1)S(1)}, bf16[3,1024,256]{2,1,0:T(8,128)(2,1)S(1)}, u32[]{:S(2)}, u32[]{:S(2)}) collective-permute-start(bf16[3,1024,256]{2,1,0:T(8,128)(2,1)S(1)} %shard_map.299.refs_2_), channel_id=1, source_target_pairs={{0,2},{2,0},{4,6},{6,4},{8,10},{10,8},{12,14},{14,12},{16,18},{18,... | collective-permute-start | bytes 4718600 | tf_op jit(solution)/shard_map/ppermute | solution.py:704
  63.2 29.3 %collective-permute-start.10 = (bf16[3,256,1024]{2,1,0:T(8,128)(2,1)S(1)}, bf16[3,256,1024]{2,1,0:T(8,128)(2,1)S(1)}, u32[]{:S(2)}, u32[]{:S(2)}) collective-permute-start(bf16[3,256,1024]{2,1,0:T(8,128)(2,1)S(1)} %shard_map.302.refs_6_), channel_id=1, source_target_pairs={{0,2},{2,0},{4,6},{6,4},{8,10},{10,8},{12,14},{14,12},{16,18},{18,... | collective-permute-start | bytes 4718600 | tf_op jit(solution)/shard_map/ppermute | solution.py:704
  63.5 14.8 %collective-permute-start.11 = (bf16[256,1024]{1,0:T(8,128)(2,1)S(1)}, bf16[256,1024]{1,0:T(8,128)(2,1)S(1)}, u32[]{:S(2)}, u32[]{:S(2)}) collective-permute-start(bf16[256,1024]{1,0:T(8,128)(2,1)S(1)} %copy-done.53), channel_id=1, source_target_pairs={{0,1},{1,0},{2,3},{3,2},{4,5},{5,4},{6,7},{7,6},{8,9},{9,8},{10,11... | collective-permute-start | bytes 1572872 | tf_op jit(solution)/shard_map/ppermute | solution.py:704
  63.8 25.0 %collective-permute-start.8 = (bf16[1024,256]{1,0:T(8,128)(2,1)S(1)}, bf16[1024,256]{1,0:T(8,128)(2,1)S(1)}, u32[]{:S(2)}, u32[]{:S(2)}) collective-permute-start(bf16[1024,256]{1,0:T(8,128)(2,1)S(1)} %copy-done.52), channel_id=1, source_target_pairs={{0,1},{1,0},{2,3},{3,2},{4,5},{5,4},{6,7},{7,6},{8,9},{9,8},{10,11... | collective-permute-start | bytes 1572872 | tf_op jit(solution)/shard_map/ppermute | solution.py:704
  92.4 31.8 %collective-permute-start.15 = (bf16[512,2048]{1,0:T(8,128)(2,1)S(1)}, bf16[512,2048]{1,0:T(8,128)(2,1)}, u32[]{:S(2)}, u32[]{:S(2)}) collective-permute-start(bf16[512,2048]{1,0:T(8,128)(2,1)S(1)} %get-tuple-element.194.refs_2_.refs_6_), channel_id=1, source_target_pairs={{0,2},{2,0},{4,6},{6,4},{8,10},{10,8},{12,14},{14,12},{16,18},{18,... | collective-permute-start | bytes 6291464 | tf_op jit(solution)/shard_map/ppermute | solution.py:704
  134.7 28.3 %collective-permute-start.17 = (bf16[2,2,4,64,512]{4,3,2,1,0:T(8,128)(2,1)}, bf16[2,2,4,64,512]{4,3,2,1,0:T(8,128)(2,1)}, u32[]{:S(2)}, u32[]{:S(2)}) collective-permute-start(bf16[2,2,4,64,512]{4,3,2,1,0:T(8,128)(2,1)} %bitcast.17), channel_id=1, source_target_pairs={{0,4},{2,6},{4,0},{6,2},{8,12},{10,14},{12,8},{14,10},{16,20},{18,... | collective-permute-start | bytes 3145736 | tf_op jit(solution)/shard_map/ppermute | solution.py:704
  136.2 26.8 %collective-permute-start.16 = (bf16[1,2,8,64,512]{4,3,2,1,0:T(8,128)(2,1)}, bf16[1,2,8,64,512]{4,3,2,1,0:T(8,128)(2,1)}, u32[]{:S(2)}, u32[]{:S(2)}) collective-permute-start(bf16[1,2,8,64,512]{4,3,2,1,0:T(8,128)(2,1)} %bitcast.15), channel_id=1, source_target_pairs={{0,1},{1,0},{2,3},{3,2},{4,5},{5,4},{6,7},{7,6},{8,9},{9,8},{10,11... | collective-permute-start | bytes 3145736 | tf_op jit(solution)/shard_map/ppermute | solution.py:704
  137.4 34.0 %collective-permute-start.20 = (bf16[8,64,512]{2,1,0:T(8,128)(2,1)}, bf16[8,64,512]{2,1,0:T(8,128)(2,1)}, u32[]{:S(2)}, u32[]{:S(2)}) collective-permute-start(bf16[8,64,512]{2,1,0:T(8,128)(2,1)} %copy-done.36), channel_id=1, source_target_pairs={{0,2},{2,0},{4,6},{6,4},{8,10},{10,8},{12,14},{14,12},{16,18},{18,... | collective-permute-start | bytes 1572872 | tf_op jit(solution)/shard_map/ppermute | solution.py:704
  151.6 19.8 %collective-permute-start.21 = (bf16[512,2048]{1,0:T(8,128)(2,1)}, bf16[512,2048]{1,0:T(8,128)(2,1)}, u32[]{:S(2)}, u32[]{:S(2)}) collective-permute-start(bf16[512,2048]{1,0:T(8,128)(2,1)} %get-tuple-element.219.refs_2_.refs_4_), channel_id=1, source_target_pairs={{0,2},{2,0},{4,6},{6,4},{8,10},{10,8},{12,14},{14,12},{16,18},{18,... | collective-permute-start | bytes 6291464 | tf_op jit(solution)/shard_map/ppermute | solution.py:704
  168.0 25.0 %collective-permute-start.18 = (bf16[1,2,4,64,512]{4,3,2,1,0:T(8,128)(2,1)}, bf16[1,2,4,64,512]{4,3,2,1,0:T(8,128)(2,1)}, u32[]{:S(2)}, u32[]{:S(2)}) collective-permute-start(bf16[1,2,4,64,512]{4,3,2,1,0:T(8,128)(2,1)} %bitcast.23), channel_id=1, source_target_pairs={{0,8},{2,10},{4,12},{6,14},{8,0},{10,2},{12,4},{14,6},{16,24},{18,... | collective-permute-start | bytes 1572872 | tf_op jit(solution)/shard_map/ppermute | solution.py:704
  169.7 24.3 %collective-permute-start.19 = (bf16[2,2,2,64,512]{4,3,2,1,0:T(8,128)(2,1)}, bf16[2,2,2,64,512]{4,3,2,1,0:T(8,128)(2,1)}, u32[]{:S(2)}, u32[]{:S(2)}) collective-permute-start(bf16[2,2,2,64,512]{4,3,2,1,0:T(8,128)(2,1)} %bitcast.25), channel_id=1, source_target_pairs={{0,8},{2,10},{4,12},{6,14},{8,0},{10,2},{12,4},{14,6},{16,24},{18,... | collective-permute-start | bytes 1572872 | tf_op jit(solution)/shard_map/ppermute | solution.py:704
  171.4 64.0 %collective-permute-start.28 = (bf16[8,64,512]{2,1,0:T(8,128)(2,1)}, bf16[8,64,512]{2,1,0:T(8,128)(2,1)}, u32[]{:S(2)}, u32[]{:S(2)}) collective-permute-start(bf16[8,64,512]{2,1,0:T(8,128)(2,1)} %get-tuple-element.273), channel_id=1, source_target_pairs={{0,2},{2,0},{4,6},{6,4},{8,10},{10,8},{12,14},{14,12},{16,18},{18,... | collective-permute-start | bytes 1572872 | tf_op jit(solution)/shard_map/ppermute | solution.py:704
  171.4 81.9 %collective-permute-start.27 = (bf16[8,64,512]{2,1,0:T(8,128)(2,1)}, bf16[8,64,512]{2,1,0:T(8,128)(2,1)}, u32[]{:S(2)}, u32[]{:S(2)}) collective-permute-start(bf16[8,64,512]{2,1,0:T(8,128)(2,1)} %get-tuple-element.271), channel_id=1, source_target_pairs={{0,2},{2,0},{4,6},{6,4},{8,10},{10,8},{12,14},{14,12},{16,18},{18,... | collective-permute-start | bytes 1572872 | tf_op jit(solution)/shard_map/ppermute | solution.py:704
  193.9 27.5 %collective-permute-start.26 = (bf16[2,2,4,64,512]{4,3,2,1,0:T(8,128)(2,1)}, bf16[2,2,4,64,512]{4,3,2,1,0:T(8,128)(2,1)}, u32[]{:S(2)}, u32[]{:S(2)}) collective-permute-start(bf16[2,2,4,64,512]{4,3,2,1,0:T(8,128)(2,1)} %bitcast.37), channel_id=1, source_target_pairs={{0,4},{2,6},{4,0},{6,2},{8,12},{10,14},{12,8},{14,10},{16,20},{18,... | collective-permute-start | bytes 3145736 | tf_op jit(solution)/shard_map/ppermute | solution.py:704
  194.3 27.5 %collective-permute-start.25 = (bf16[1,2,8,64,512]{4,3,2,1,0:T(8,128)(2,1)}, bf16[1,2,8,64,512]{4,3,2,1,0:T(8,128)(2,1)}, u32[]{:S(2)}, u32[]{:S(2)}) collective-permute-start(bf16[1,2,8,64,512]{4,3,2,1,0:T(8,128)(2,1)} %bitcast.35), channel_id=1, source_target_pairs={{0,1},{1,0},{2,3},{3,2},{4,5},{5,4},{6,7},{7,6},{8,9},{9,8},{10,11... | collective-permute-start | bytes 3145736 | tf_op jit(solution)/shard_map/ppermute | solution.py:704
  200.6 26.1 %collective-permute-start.23 = (bf16[1,2,2,64,512]{4,3,2,1,0:T(8,128)(2,1)}, bf16[1,2,2,64,512]{4,3,2,1,0:T(8,128)(2,1)}, u32[]{:S(2)}, u32[]{:S(2)}) collective-permute-start(bf16[1,2,2,64,512]{4,3,2,1,0:T(8,128)(2,1)} %bitcast.31), channel_id=1, source_target_pairs={{0,16},{2,18},{4,20},{6,22},{8,24},{10,26},{12,28},{14,30},{16,0},... | collective-permute-start | bytes 786440 | tf_op jit(solution)/shard_map/ppermute | solution.py:704
  221.8 33.2 %collective-permute-start.29 = (bf16[3,512,1024]{2,1,0:T(8,128)(2,1)}, bf16[3,512,1024]{2,1,0:T(8,128)(2,1)}, u32[]{:S(2)}, u32[]{:S(2)}) collective-permute-start(bf16[3,512,1024]{2,1,0:T(8,128)(2,1)} %get-tuple-element.265.g_qkv.refs_4_.refs_8_), channel_id=1, source_target_pairs={{0,2},{2,0},{4,6},{6,4},{8,10},{10,8},{12,14},{14,12},{16,18},{18,... | collective-permute-start | bytes 9437192 | tf_op jit(solution)/shard_map/ppermute | solution.py:704
  226.7 26.6 %collective-permute-start.30 = (bf16[512,1024]{1,0:T(8,128)(2,1)S(1)}, bf16[512,1024]{1,0:T(8,128)(2,1)S(1)}, u32[]{:S(2)}, u32[]{:S(2)}) collective-permute-start(bf16[512,1024]{1,0:T(8,128)(2,1)S(1)} %get-tuple-element.274.refs_6_), channel_id=1, source_target_pairs={{0,2},{2,0},{4,6},{6,4},{8,10},{10,8},{12,14},{14,12},{16,18},{18,... | collective-permute-start | bytes 3145736 | tf_op jit(solution)/shard_map/ppermute | solution.py:704
  235.3 31.5 %collective-permute-start.36 = (bf16[1,2,4,64,512]{4,3,2,1,0:T(8,128)(2,1)S(1)}, bf16[1,2,4,64,512]{4,3,2,1,0:T(8,128)(2,1)S(1)}, u32[]{:S(2)}, u32[]{:S(2)}) collective-permute-start(bf16[1,2,4,64,512]{4,3,2,1,0:T(8,128)(2,1)S(1)} %bitcast.162), channel_id=1, source_target_pairs={{0,8},{2,10},{4,12},{6,14},{8,0},{10,2},{12,4},{14,6},{16,24},{18,... | collective-permute-start | bytes 1572872 | tf_op jit(solution)/shard_map/ppermute | solution.py:704
  235.3 31.5 %collective-permute-start.37 = (bf16[2,2,2,64,512]{4,3,2,1,0:T(8,128)(2,1)S(1)}, bf16[2,2,2,64,512]{4,3,2,1,0:T(8,128)(2,1)S(1)}, u32[]{:S(2)}, u32[]{:S(2)}) collective-permute-start(bf16[2,2,2,64,512]{4,3,2,1,0:T(8,128)(2,1)S(1)} %bitcast.161), channel_id=1, source_target_pairs={{0,8},{2,10},{4,12},{6,14},{8,0},{10,2},{12,4},{14,6},{16,24},{18,... | collective-permute-start | bytes 1572872 | tf_op jit(solution)/shard_map/ppermute | solution.py:704
  253.3 15.5 %collective-permute-start.33 = (f32[12288]{0:T(1024)}, f32[12288]{0:T(1024)}, u32[]{:S(2)}, u32[]{:S(2)}) collective-permute-start(f32[12288]{0:T(1024)} %bitcast_dynamic-update-slice_fusion), channel_id=1, source_target_pairs={{0,2},{2,0},{4,6},{6,4},{8,10},{10,8},{12,14},{14,12},{16,18},{18,... | collective-permute-start | bytes 147464 | tf_op jit(solution)/shard_map/ppermute | solution.py:704
  269.6 19.8 %collective-permute-start.39 = (bf16[1,2,2,64,512]{4,3,2,1,0:T(8,128)(2,1)S(1)}, bf16[1,2,2,64,512]{4,3,2,1,0:T(8,128)(2,1)S(1)}, u32[]{:S(2)}, u32[]{:S(2)}) collective-permute-start(bf16[1,2,2,64,512]{4,3,2,1,0:T(8,128)(2,1)S(1)} %bitcast.172), channel_id=1, source_target_pairs={{0,16},{2,18},{4,20},{6,22},{8,24},{10,26},{12,28},{14,30},{16,0},... | collective-permute-start | bytes 786440 | tf_op jit(solution)/shard_map/ppermute | solution.py:704
  269.6 25.3 %collective-permute-start.40 = (bf16[2,2,1,64,512]{4,3,1,0,2:T(8,128)(2,1)S(1)}, bf16[2,2,1,64,512]{4,3,1,0,2:T(8,128)(2,1)S(1)}, u32[]{:S(2)}, u32[]{:S(2)}) collective-permute-start(bf16[2,2,1,64,512]{4,3,1,0,2:T(8,128)(2,1)S(1)} %bitcast.171), channel_id=1, source_target_pairs={{0,16},{2,18},{4,20},{6,22},{8,24},{10,26},{12,28},{14,30},{16,0},... | collective-permute-start | bytes 786440 | tf_op jit(solution)/shard_map/ppermute | solution.py:704
  272.6 23.2 %collective-permute-start.38 = (f32[12288]{0:T(1024)S(1)}, f32[12288]{0:T(1024)S(1)}, u32[]{:S(2)}, u32[]{:S(2)}) collective-permute-start(f32[12288]{0:T(1024)S(1)} %add.60), channel_id=1, source_target_pairs={{0,4},{2,6},{4,0},{6,2},{8,12},{10,14},{12,8},{14,10},{16,20},{18,... | collective-permute-start | bytes 147464 | tf_op jit(solution)/shard_map/ppermute | solution.py:704
  273.2 24.7 %collective-permute-start.31 = (bf16[1,2,8,64,512]{4,3,2,1,0:T(8,128)(2,1)S(1)}, bf16[1,2,8,64,512]{4,3,2,1,0:T(8,128)(2,1)S(1)}, u32[]{:S(2)}, u32[]{:S(2)}) collective-permute-start(bf16[1,2,8,64,512]{4,3,2,1,0:T(8,128)(2,1)S(1)} %get-tuple-element.368), channel_id=1, source_target_pairs={{0,1},{1,0},{2,3},{3,2},{4,5},{5,4},{6,7},{7,6},{8,9},{9,8},{10,11... | collective-permute-start | bytes 3145736 | tf_op jit(solution)/shard_map/ppermute | solution.py:704
  274.9 24.7 %collective-permute-start.32 = (bf16[2,2,4,64,512]{4,3,2,1,0:T(8,128)(2,1)S(1)}, bf16[2,2,4,64,512]{4,3,2,1,0:T(8,128)(2,1)S(1)}, u32[]{:S(2)}, u32[]{:S(2)}) collective-permute-start(bf16[2,2,4,64,512]{4,3,2,1,0:T(8,128)(2,1)S(1)} %bitcast.210), channel_id=1, source_target_pairs={{0,4},{2,6},{4,0},{6,2},{8,12},{10,14},{12,8},{14,10},{16,20},{18,... | collective-permute-start | bytes 3145736 | tf_op jit(solution)/shard_map/ppermute | solution.py:704
  (85 other events, 711.1 us)
